TPU v7x, 32 devices: a whole 2x2x4 slice. The times are simulated.
32 devices in a mesh: dp: 8 (over z, x), fsdp: 4 (over y, core).
Axes of the slice: x: 2, y: 2, z: 4, core: 2. Of those that a mesh axis runs over, the one named last changes fastest.
Arguments:
- tokens: bfloat16 [65536, 512], P(('dp', 'fsdp')), may hold values from -6 to 6
- lengths: int32 [64], P(('dp', 'fsdp')), may hold values from 640 to 1024, as said below
- norm_gains: bfloat16 [2, 512], P(None, 'fsdp'), may hold values from 0.25 to 1.75
- ema_params: bfloat16 [4, 512, 16], P(None, 'fsdp'), may hold values from -5 to 3
- qk_affine: bfloat16 [4, 128], P(None, 'fsdp'), may hold values from -2 to 2
- w_z: bfloat16 [512, 128], P('fsdp'), may hold values from -0.25 to 0.25
- w_v: bfloat16 [512, 1024], P('fsdp'), may hold values from -0.25 to 0.25
- w_r: bfloat16 [512, 1024], P('fsdp'), may hold values from -0.25 to 0.25
- w_u: bfloat16 [512, 512], P('fsdp'), may hold values from -0.25 to 0.25
- w_h: bfloat16 [512, 512], P('fsdp'), may hold values from -0.25 to 0.25
- u_h: bfloat16 [1024, 512], P('fsdp'), may hold values from -0.5 to 0.5
- w_in: bfloat16 [512, 1024], P('fsdp'), may hold values from -0.25 to 0.25
- w_out: bfloat16 [1024, 512], P('fsdp'), may hold values from -0.1875 to 0.1875
- cotangent: bfloat16 [65536, 512], P(('dp', 'fsdp')), may hold values from -6 to 6
Outputs:
- output: bfloat16 [65536, 512], P(('dp', 'fsdp'))
- grad_tokens: bfloat16 [65536, 512], P(('dp', 'fsdp'))
- grad_norm_gains: float32 [2, 512], P(None, 'fsdp')
- grad_ema_params: float32 [4, 512, 16], P(None, 'fsdp')
- grad_qk_affine: float32 [4, 128], P(None, 'fsdp')
- grad_w_z: float32 [512, 128], P('fsdp')
- grad_w_v: float32 [512, 1024], P('fsdp')
- grad_w_r: float32 [512, 1024], P('fsdp')
- grad_w_u: float32 [512, 512], P('fsdp')
- grad_w_h: float32 [512, 512], P('fsdp')
- grad_u_h: float32 [1024, 512], P('fsdp')
- grad_w_in: float32 [512, 1024], P('fsdp')
- grad_w_out: float32 [1024, 512], P('fsdp')
Inputs may be any that keep to these rules, and one draw needn't show every extreme that they name: `lengths`: some slot holds 1024 valid tokens in every draw.
All inputs are finite; a program needn't handle non-finite values.
Results may differ from a plain program's by a relative error of at most 0.038.
Values may be sent and summed in bfloat16 or wider, within the bound.
A program may use at most 320 MiB of HBM per device.

v0:
```python
import jax
import jax.numpy as jnp
from jax import lax
from jax.sharding import PartitionSpec as P

SPAN = 128


epsilon = 1e-06
highest = lax.Precision.HIGHEST


def silu_act(inputs):
    return inputs * jax.nn.sigmoid(inputs)


def silu_slope(inputs):
    sigma = jax.nn.sigmoid(inputs)
    return sigma * (1.0 + inputs * (1.0 - sigma))


def normalize(values, scales):
    mean_sq = jnp.mean(values * values, axis=-1, keepdims=True)
    return values * lax.rsqrt(mean_sq + epsilon) * scales


def smooth(inputs, params):
    batch_size, seq_length, model_width = inputs.shape
    block_count = seq_length // SPAN
    rate_in = jax.nn.sigmoid(params[0])
    damping = jax.nn.sigmoid(params[1])
    expand = params[2]
    readout = params[3]
    retain = 1.0 - rate_in * damping
    log_keep = jnp.log(retain)
    offsets = jnp.arange(SPAN).astype(inputs.dtype)
    powers = jnp.exp(offsets[:, None, None] * log_keep[None])
    kernel = jnp.einsum("tjh,jh->jt", powers, rate_in * expand * readout, precision=highest)
    lag_table = jnp.arange(SPAN)[:, None] - jnp.arange(SPAN)[None, :]
    toeplitz = jnp.where(
        lag_table[None] >= 0, jnp.take(kernel, jnp.maximum(lag_table, 0), axis=1), 0.0
    )
    emit_table = powers * retain[None] * readout[None]
    absorb_table = powers[::-1] * (rate_in * expand)[None]
    carry_decay = powers[-1] * retain
    pieces = inputs.reshape(batch_size, block_count, SPAN, model_width)
    local_part = jnp.einsum("jts,bcsj->bctj", toeplitz, pieces, precision=highest)

    def advance(state_in, block_in):
        following = state_in * carry_decay[None] + jnp.einsum(
            "sjh,bsj->bjh", absorb_table, block_in, precision=highest
        )
        return (following, state_in)

    ordered = jnp.swapaxes(pieces, 0, 1)
    initial = jnp.zeros((batch_size, model_width, params.shape[-1]), inputs.dtype)
    unused, states = lax.scan(jax.checkpoint(advance), initial, ordered)
    carried = jnp.einsum("tjh,cbjh->bctj", emit_table, states, precision=highest)
    return (local_part + carried).reshape(batch_size, seq_length, model_width)


def matmul(left, right):
    return jnp.dot(left, right, preferred_element_type=jnp.float32)


def matmul_left_t(left, right):
    return lax.dot_general(
        left, right, (((0,), (0,)), ((), ())), preferred_element_type=jnp.float32
    )


def matmul_right_t(left, right):
    return lax.dot_general(
        left, right, (((1,), (1,)), ((), ())), preferred_element_type=jnp.float32
    )


def per_device(
    tokens,
    lengths,
    norm_gains,
    ema_params,
    qk_affine,
    w_z,
    w_v,
    w_r,
    w_u,
    w_h,
    u_h,
    w_in,
    w_out,
    cotangent,
):
    shards = (norm_gains, ema_params, qk_affine, w_z, w_v, w_r, w_u, w_h, u_h, w_in, w_out)
    fetched = (
        lax.all_gather(shards[0], "fsdp", axis=1, tiled=True),
        lax.all_gather(shards[1], "fsdp", axis=1, tiled=True),
        lax.all_gather(shards[2], "fsdp", axis=1, tiled=True),
        lax.all_gather(shards[3], "fsdp", axis=0, tiled=True),
        lax.all_gather(shards[4], "fsdp", axis=0, tiled=True),
        lax.all_gather(shards[5], "fsdp", axis=0, tiled=True),
        lax.all_gather(shards[6], "fsdp", axis=0, tiled=True),
        lax.all_gather(shards[7], "fsdp", axis=0, tiled=True),
        lax.all_gather(shards[8], "fsdp", axis=0, tiled=True),
        lax.all_gather(shards[9], "fsdp", axis=0, tiled=True),
        lax.all_gather(shards[10], "fsdp", axis=0, tiled=True),
    )
    (
        gain_rows,
        ema_table,
        affine,
        weight_z,
        weight_v,
        weight_r,
        weight_u,
        weight_h,
        weight_uh,
        weight_in,
        weight_out,
    ) = fetched
    seq_count = lengths.shape[0]
    row_count, model_width = tokens.shape
    seq_length = row_count // seq_count
    block_count = seq_length // SPAN
    gains_full = gain_rows.astype(jnp.float32)
    ema_full = ema_table.astype(jnp.float32)
    affine_full = affine.astype(jnp.float32)
    positions = jnp.arange(seq_length, dtype=jnp.int32)
    valid = positions[None, :] < lengths[:, None]
    row_valid = valid.reshape(row_count, 1).astype(jnp.float32)
    key_valid = valid.reshape(seq_count, block_count, 1, SPAN)
    inputs = tokens.astype(jnp.float32)
    normed, norm_back = jax.vjp(normalize, inputs, gains_full[0])
    smoothed, smooth_back = jax.vjp(
        smooth, normed.reshape(seq_count, seq_length, model_width), ema_full
    )
    smoothed = smoothed.reshape(row_count, model_width)
    normed_low = normed.astype(jnp.bfloat16)
    smooth_low = smoothed.astype(jnp.bfloat16)
    shared_pre = matmul(smooth_low, weight_z)
    value_pre = matmul(normed_low, weight_v)
    reset_pre = matmul(smooth_low, weight_r)
    update_pre = matmul(smooth_low, weight_u)
    shared = silu_act(shared_pre)
    queries = (shared * affine_full[0] + affine_full[1]).astype(jnp.bfloat16)
    keys_low = (shared * affine_full[2] + affine_full[3]).astype(jnp.bfloat16)
    values_low = silu_act(value_pre).astype(jnp.bfloat16)
    score_scale = shared_pre.shape[1] ** (-0.5)
    query_blocks = queries.reshape(seq_count, block_count, SPAN, -1)
    key_blocks = keys_low.reshape(seq_count, block_count, SPAN, -1)
    value_blocks = values_low.reshape(seq_count, block_count, SPAN, -1)

    def masked_scores():
        scores = (
            jnp.einsum(
                "bctz,bcsz->bcts", query_blocks, key_blocks, preferred_element_type=jnp.float32
            )
            * score_scale
        )
        return jnp.where(key_valid, scores, -1000000000.0)

    first_scores = masked_scores()
    row_max = jnp.max(first_scores, axis=-1, keepdims=True)
    exp_scores = jnp.exp(first_scores - row_max)
    row_total = jnp.sum(exp_scores, axis=-1, keepdims=True)
    log_total = row_max + jnp.log(row_total)
    probs = exp_scores / row_total
    attended = (
        jnp.einsum(
            "bcts,bcsv->bctv",
            probs.astype(jnp.bfloat16),
            value_blocks,
            preferred_element_type=jnp.float32,
        ).reshape(row_count, -1)
        * row_valid
    )
    reset = silu_act(reset_pre)
    update = jax.nn.sigmoid(update_pre)
    gated_low = (reset * attended).astype(jnp.bfloat16)
    hidden_pre = matmul(smooth_low, weight_h) + matmul(gated_low, weight_uh)
    candidate = silu_act(hidden_pre)
    middle = inputs + update * (candidate - inputs)
    ffn_norm, ffn_back = jax.vjp(normalize, middle, gains_full[1])
    ffn_low = ffn_norm.astype(jnp.bfloat16)
    ffn_pre = matmul(ffn_low, weight_in)
    ffn_act = silu_act(ffn_pre).astype(jnp.bfloat16)
    output = (middle + matmul(ffn_act, weight_out)).astype(jnp.bfloat16)
    again = (
        lax.all_gather(qk_affine, "fsdp", axis=1, tiled=True),
        lax.all_gather(w_z, "fsdp", axis=0, tiled=True),
        lax.all_gather(w_v, "fsdp", axis=0, tiled=True),
        lax.all_gather(w_r, "fsdp", axis=0, tiled=True),
        lax.all_gather(w_u, "fsdp", axis=0, tiled=True),
        lax.all_gather(w_h, "fsdp", axis=0, tiled=True),
        lax.all_gather(u_h, "fsdp", axis=0, tiled=True),
        lax.all_gather(w_in, "fsdp", axis=0, tiled=True),
        lax.all_gather(w_out, "fsdp", axis=0, tiled=True),
    )
    back_affine, back_z, back_v, back_r, back_u, back_h, back_uh, back_in, back_out = again
    back_affine = back_affine.astype(jnp.float32)
    grad_out_w = matmul_left_t(ffn_act, cotangent)
    grad_act = matmul_right_t(cotangent, back_out)
    grad_ffn_pre = (grad_act * silu_slope(ffn_pre)).astype(jnp.bfloat16)
    grad_in_w = matmul_left_t(ffn_low, grad_ffn_pre)
    grad_ffn_norm = matmul_right_t(grad_ffn_pre, back_in)
    grad_middle, grad_gain_second = ffn_back(grad_ffn_norm)
    grad_middle = grad_middle + cotangent.astype(jnp.float32)
    grad_inputs = grad_middle * (1.0 - update)
    grad_update = grad_middle * (candidate - inputs)
    grad_hidden = (grad_middle * update * silu_slope(hidden_pre)).astype(jnp.bfloat16)
    grad_h_w = matmul_left_t(smooth_low, grad_hidden)
    grad_uh_w = matmul_left_t(gated_low, grad_hidden)
    grad_smooth = matmul_right_t(grad_hidden, back_h)
    grad_gated = matmul_right_t(grad_hidden, back_uh)
    grad_reset_pre = (grad_gated * attended * silu_slope(reset_pre)).astype(jnp.bfloat16)
    grad_update_pre = (grad_update * update * (1.0 - update)).astype(jnp.bfloat16)
    grad_attended = (grad_gated * reset * row_valid).astype(jnp.bfloat16)
    again_probs = jnp.exp(masked_scores() - log_total)
    grad_blocks = grad_attended.reshape(seq_count, block_count, SPAN, -1)
    grad_probs = jnp.einsum(
        "bctv,bcsv->bcts", grad_blocks, value_blocks, preferred_element_type=jnp.float32
    )
    row_inner = jnp.sum(grad_probs * again_probs, axis=-1, keepdims=True)
    grad_scores = (again_probs * (grad_probs - row_inner)).astype(jnp.bfloat16)
    grad_queries = (
        jnp.einsum(
            "bcts,bcsz->bctz", grad_scores, key_blocks, preferred_element_type=jnp.float32
        ).reshape(row_count, -1)
        * score_scale
    )
    grad_keys = (
        jnp.einsum(
            "bcts,bctz->bcsz", grad_scores, query_blocks, preferred_element_type=jnp.float32
        ).reshape(row_count, -1)
        * score_scale
    )
    grad_values = jnp.einsum(
        "bcts,bctv->bcsv",
        again_probs.astype(jnp.bfloat16),
        grad_blocks,
        preferred_element_type=jnp.float32,
    ).reshape(row_count, -1)
    grad_value_pre = (grad_values * silu_slope(value_pre)).astype(jnp.bfloat16)
    grad_affine = jnp.stack(
        [
            jnp.sum(grad_queries * shared, axis=0),
            jnp.sum(grad_queries, axis=0),
            jnp.sum(grad_keys * shared, axis=0),
            jnp.sum(grad_keys, axis=0),
        ]
    )
    grad_shared = grad_queries * back_affine[0] + grad_keys * back_affine[2]
    grad_shared_pre = (grad_shared * silu_slope(shared_pre)).astype(jnp.bfloat16)
    grad_z_w = matmul_left_t(smooth_low, grad_shared_pre)
    grad_v_w = matmul_left_t(normed_low, grad_value_pre)
    grad_r_w = matmul_left_t(smooth_low, grad_reset_pre)
    grad_u_w = matmul_left_t(smooth_low, grad_update_pre)
    grad_smooth = (
        grad_smooth
        + matmul_right_t(grad_shared_pre, back_z)
        + matmul_right_t(grad_reset_pre, back_r)
        + matmul_right_t(grad_update_pre, back_u)
    )
    grad_normed, grad_ema = smooth_back(grad_smooth.reshape(seq_count, seq_length, model_width))
    grad_normed = grad_normed.reshape(row_count, model_width) + matmul_right_t(
        grad_value_pre, back_v
    )
    grad_direct, grad_gain_first = norm_back(grad_normed)
    grad_tokens = (grad_inputs + grad_direct).astype(jnp.bfloat16)
    grad_gains = jnp.stack([grad_gain_first, grad_gain_second])
    totals = (
        grad_gains,
        grad_ema,
        grad_affine,
        grad_z_w,
        grad_v_w,
        grad_r_w,
        grad_u_w,
        grad_h_w,
        grad_uh_w,
        grad_in_w,
        grad_out_w,
    )
    summed = lax.psum(
        (
            totals[0],
            totals[1],
            totals[2],
            totals[3],
            totals[4],
            totals[5],
            totals[6],
            totals[7],
            totals[8],
            totals[9],
            totals[10],
        ),
        ("dp", "fsdp"),
    )
    shard_index = lax.axis_index("fsdp")
    shard_total = lax.axis_size("fsdp")
    pieces = tuple(
        (
            lax.dynamic_slice_in_dim(
                summed_grad,
                shard_index * (summed_grad.shape[grad_dim] // shard_total),
                summed_grad.shape[grad_dim] // shard_total,
                grad_dim,
            )
            for summed_grad, grad_dim in zip(summed, (1, 1, 1, 0, 0, 0, 0, 0, 0, 0, 0))
        )
    )
    return (output, grad_tokens) + tuple(pieces)


def solution(mesh):
    return jax.shard_map(
        per_device,
        mesh=mesh,
        in_specs=(
            P(("dp", "fsdp"), None),
            P(("dp", "fsdp")),
            P(None, "fsdp"),
            P(None, "fsdp", None),
            P(None, "fsdp"),
            P("fsdp", None),
            P("fsdp", None),
            P("fsdp", None),
            P("fsdp", None),
            P("fsdp", None),
            P("fsdp", None),
            P("fsdp", None),
            P("fsdp", None),
            P(("dp", "fsdp"), None),
        ),
        out_specs=(
            P(("dp", "fsdp"), None),
            P(("dp", "fsdp"), None),
            P(None, "fsdp"),
            P(None, "fsdp", None),
            P(None, "fsdp"),
            P("fsdp", None),
            P("fsdp", None),
            P("fsdp", None),
            P("fsdp", None),
            P("fsdp", None),
            P("fsdp", None),
            P("fsdp", None),
            P("fsdp", None),
        ),
        check_vma=False,
    )
```

profile of v0, /device:TPU:0, one launch (start us, length us, event | category | flops | bytes accessed | tf_op | source)
XLA Modules:
  0.0 1259.7 jit_solution(15750464863962594139)
XLA Ops:
  10.7 6.5 all_gather.43
  20.6 5.3 all-gather
  30.7 5.0 all_gather.42
  36.8 6.3 all_gather.47
  45.9 5.9 copy.365
  53.3 4.3 copy.465
  61.2 5.8 copy.322
  67.0 83.8 %while.34 = (s32[]{:T(128)}, f32[2,512,16]{2,0,1:T(2,128)S(1)}, f32[8,2,512,16]{3,1,2,0:T(2,128)}, f32[1,512,16]{2,1,0:T(8,128)S(1)}, f32[8,2,128,512]{2,1,3,0:T...) while((s32[]{:T(128)}, f32[2,512,16]{2,0,1:T(2,128)S(1)}, ...), condition=%wide.region_2.3_spmd.clone, body=%wide.region_1.2_spmd.clone.sunk | while | flops 25231364 | bytes 5472368 | solution.py:57
  68.2 9.4 fusion.213
  78.7 9.4 fusion.213
  89.2 9.4 fusion.213
  99.6 9.4 fusion.213
  110.1 9.4 fusion.213
  120.6 9.4 fusion.213
  131.0 9.4 fusion.213
  141.5 9.4 fusion.213
  152.1 64.3 %gather_fusion = f32[16384,512]{1,0:T(8,128)} fusion(f32[512,128]{0,1:T(8,128)S(1)} %multiply_reduce_fusion.2, s32[16384]{0:T(1024)S(1)} %broadcast_clamp_fusion), kind=kCustom, calls=%fused_computation | custom fusion | bytes 67174400 | tf_op jit(solution)/shard_map/jvp(jit(_take))/gather | solution.py:41
  216.4 35.7 %copy.319 = f32[128,128,512]{1,0,2:T(8,128)} copy(f32[128,128,512]{2,1,0:T(8,128)} %bitcast.401) | data formatting | bytes 67108864 | tf_op jit(solution)/shard_map/jvp(jit(_take))/gather | solution.py:41
  252.3 8.2 all_gather.45
  260.5 7.7 all_gather.44
  270.7 9.4 fusion.45
  280.3 55.9 %fusion.42 = bf16[2,8,128,512]{2,1,0,3:T(8,128)(2,1)S(1)} fusion(f32[512,8,2,128]{3,1,2,0:T(8,128)S(1)} %fusion.45, f32[2,8,128,512]{2,1,0,3:T(8,128)S(1)} %bitcast.403, f32[128,128,512]{1,0,2:T(8,128)} %copy.319, pred[128,128]{1,0:T(8,128)(4,1)S(1)} %get-tuple-element.633, pred[128,128]{1,0:T(8,128)(4,1)S(1)} %get-tuple-element.632), kind=kOutput, calls=%fused_computation.82 | convolution fusion | flops 1629487104 | bytes 44072960 | tf_op jit(solution)/shard_map/jvp(jts,bcsj->bctj)/dot_general | solution.py:47
  341.0 7.5 multiply_convert_fusion.5
  350.5 4.6 fusion.92
  355.1 9.5 multiply_convert_fusion.4
  364.6 5.2 fusion.136
  371.3 5.8 multiply_reduce_fusion.7
  377.2 10.6 multiply_convert_fusion.3
  387.8 8.6 multiply_convert_fusion.2
  409.9 10.6 multiply_convert_fusion.1
  420.5 4.5 fusion.90
  437.3 5.6 copy.331
  442.9 12.3 fusion.47
  455.2 10.1 fusion.50
  465.3 57.0 %fusion.7 = f32[128,128,512]{1,0,2:T(8,128)} fusion(pred[128,128]{1,0:T(8,128)(4,1)S(1)} %copy-done.60, f32[2,8,128,512]{2,1,0,3:T(8,128)S(1)} %bitcast.404, f32[2,8,128,512]{2,1,0,3:T(8,128)S(1)} %copy-done.3), kind=kOutput, calls=%fused_computation.21 | convolution fusion | flops 1619001344 | bytes 41959424 | tf_op jit(solution)/shard_map/transpose(jvp(jts,bcsj->bctj))/dot_general | solution.py:47
  541.9 264.3 %while.35 = (s32[]{:T(128)}, f32[512,16]{1,0:T(8,128)S(1)}, f32[128,512,16]{0,2,1:T(8,128)}, f32[2,512,16]{2,0,1:T(2,128)S(1)}, f32[8,2,128,512]{2,0,1,3:T(8,128...) while((s32[]{:T(128)}, f32[512,16]{1,0:T(8,128)S(1)}, ...), condition=%wide.region_10.11_spmd.clone, body=%wide.region_8.10_spmd.clone.sunk | while | flops 52518916 | bytes 67010816 | solution.py:57
  548.7 8.1 bitcast_add_fusion.6
  560.5 14.5 %dynamic_update_slice.20 = f32[8,2,128,512]{2,0,1,3:T(8,128)} dynamic-update-slice(f32[8,2,128,512]{2,0,1,3:T(8,128)} %get-tuple-element.789, f32[1,2,128,512]{2,0,1,3:T(1,128)S(1)} %bitcast.405, s32[]{:T(128)S(6)} %sub.235, s32[]{:T(128)} %constant.113.clone.1..sunk.1, s32[]{:T(128)} %constant.113.clone.1..sunk.1, s32[]{:T(128)} %constant.113.clone.1..sunk.1) | dynamic-update-slice | bytes 1048580 | tf_op jit(solution)/shard_map/transpose(jvp())/while/body/jit(dynamic_update_index_in_dim)/dynamic_update_slice | solution.py:57
  581.6 8.1 bitcast_add_fusion.6
  593.5 14.5 %dynamic_update_slice.20 = f32[8,2,128,512]{2,0,1,3:T(8,128)} dynamic-update-slice(f32[8,2,128,512]{2,0,1,3:T(8,128)} %get-tuple-element.789, f32[1,2,128,512]{2,0,1,3:T(1,128)S(1)} %bitcast.405, s32[]{:T(128)S(6)} %sub.235, s32[]{:T(128)} %constant.113.clone.1..sunk.1, s32[]{:T(128)} %constant.113.clone.1..sunk.1, s32[]{:T(128)} %constant.113.clone.1..sunk.1) | dynamic-update-slice | bytes 1048580 | tf_op jit(solution)/shard_map/transpose(jvp())/while/body/jit(dynamic_update_index_in_dim)/dynamic_update_slice | solution.py:57
  614.6 8.1 bitcast_add_fusion.6
  626.4 14.5 %dynamic_update_slice.20 = f32[8,2,128,512]{2,0,1,3:T(8,128)} dynamic-update-slice(f32[8,2,128,512]{2,0,1,3:T(8,128)} %get-tuple-element.789, f32[1,2,128,512]{2,0,1,3:T(1,128)S(1)} %bitcast.405, s32[]{:T(128)S(6)} %sub.235, s32[]{:T(128)} %constant.113.clone.1..sunk.1, s32[]{:T(128)} %constant.113.clone.1..sunk.1, s32[]{:T(128)} %constant.113.clone.1..sunk.1) | dynamic-update-slice | bytes 1048580 | tf_op jit(solution)/shard_map/transpose(jvp())/while/body/jit(dynamic_update_index_in_dim)/dynamic_update_slice | solution.py:57
  647.6 8.1 bitcast_add_fusion.6
  659.4 14.5 %dynamic_update_slice.20 = f32[8,2,128,512]{2,0,1,3:T(8,128)} dynamic-update-slice(f32[8,2,128,512]{2,0,1,3:T(8,128)} %get-tuple-element.789, f32[1,2,128,512]{2,0,1,3:T(1,128)S(1)} %bitcast.405, s32[]{:T(128)S(6)} %sub.235, s32[]{:T(128)} %constant.113.clone.1..sunk.1, s32[]{:T(128)} %constant.113.clone.1..sunk.1, s32[]{:T(128)} %constant.113.clone.1..sunk.1) | dynamic-update-slice | bytes 1048580 | tf_op jit(solution)/shard_map/transpose(jvp())/while/body/jit(dynamic_update_index_in_dim)/dynamic_update_slice | solution.py:57
  680.6 8.1 bitcast_add_fusion.6
  692.4 14.5 %dynamic_update_slice.20 = f32[8,2,128,512]{2,0,1,3:T(8,128)} dynamic-update-slice(f32[8,2,128,512]{2,0,1,3:T(8,128)} %get-tuple-element.789, f32[1,2,128,512]{2,0,1,3:T(1,128)S(1)} %bitcast.405, s32[]{:T(128)S(6)} %sub.235, s32[]{:T(128)} %constant.113.clone.1..sunk.1, s32[]{:T(128)} %constant.113.clone.1..sunk.1, s32[]{:T(128)} %constant.113.clone.1..sunk.1) | dynamic-update-slice | bytes 1048580 | tf_op jit(solution)/shard_map/transpose(jvp())/while/body/jit(dynamic_update_index_in_dim)/dynamic_update_slice | solution.py:57
  713.5 8.1 bitcast_add_fusion.6
  725.4 14.5 %dynamic_update_slice.20 = f32[8,2,128,512]{2,0,1,3:T(8,128)} dynamic-update-slice(f32[8,2,128,512]{2,0,1,3:T(8,128)} %get-tuple-element.789, f32[1,2,128,512]{2,0,1,3:T(1,128)S(1)} %bitcast.405, s32[]{:T(128)S(6)} %sub.235, s32[]{:T(128)} %constant.113.clone.1..sunk.1, s32[]{:T(128)} %constant.113.clone.1..sunk.1, s32[]{:T(128)} %constant.113.clone.1..sunk.1) | dynamic-update-slice | bytes 1048580 | tf_op jit(solution)/shard_map/transpose(jvp())/while/body/jit(dynamic_update_index_in_dim)/dynamic_update_slice | solution.py:57
  746.5 8.1 bitcast_add_fusion.6
  758.3 14.5 %dynamic_update_slice.20 = f32[8,2,128,512]{2,0,1,3:T(8,128)} dynamic-update-slice(f32[8,2,128,512]{2,0,1,3:T(8,128)} %get-tuple-element.789, f32[1,2,128,512]{2,0,1,3:T(1,128)S(1)} %bitcast.405, s32[]{:T(128)S(6)} %sub.235, s32[]{:T(128)} %constant.113.clone.1..sunk.1, s32[]{:T(128)} %constant.113.clone.1..sunk.1, s32[]{:T(128)} %constant.113.clone.1..sunk.1) | dynamic-update-slice | bytes 1048580 | tf_op jit(solution)/shard_map/transpose(jvp())/while/body/jit(dynamic_update_index_in_dim)/dynamic_update_slice | solution.py:57
  779.5 8.1 bitcast_add_fusion.6
  791.3 14.5 %dynamic_update_slice.20 = f32[8,2,128,512]{2,0,1,3:T(8,128)} dynamic-update-slice(f32[8,2,128,512]{2,0,1,3:T(8,128)} %get-tuple-element.789, f32[1,2,128,512]{2,0,1,3:T(1,128)S(1)} %bitcast.405, s32[]{:T(128)S(6)} %sub.235, s32[]{:T(128)} %constant.113.clone.1..sunk.1, s32[]{:T(128)} %constant.113.clone.1..sunk.1, s32[]{:T(128)} %constant.113.clone.1..sunk.1) | dynamic-update-slice | bytes 1048580 | tf_op jit(solution)/shard_map/transpose(jvp())/while/body/jit(dynamic_update_index_in_dim)/dynamic_update_slice | solution.py:57
  806.2 5.6 copy.341
  811.8 34.8 %copy.383 = f32[128,128,512]{2,1,0:T(8,128)} copy(f32[128,128,512]{1,0,2:T(8,128)} %fusion.7) | data formatting | bytes 67108864 | tf_op jit(solution)/shard_map/transpose(jvp(jit(_where)))/select_n | solution.py:40
  846.6 5.6 copy.345
  852.3 7.4 broadcast_multiply_fusion
  860.4 104.4 %scatter_custom_fusion = f32[512,128]{0,1:T(8,128)S(1)} fusion(s32[16384]{0:T(1024)} %maximum_bitcast_fusion, f32[16384,512]{1,0:T(8,128)} %bitcast.407, f32[]{:T(128)} %constant.110.clone.1), kind=kCustom, calls=%fused_computation.165 | custom fusion | flops 8388608 | bytes 262656 | tf_op jit(solution)/shard_map/transpose(jvp(jit(_take)))/scatter-add | solution.py:41
  965.6 7.5 fusion.20
  990.4 7.8 add_convert_fusion
  1002.3 33.8 %bitcast_add_fusion.3 = f32[2,8,128,512]{2,1,0,3:T(8,128)S(1)} fusion(f32[8,2,128,512]{2,0,1,3:T(8,128)} %get-tuple-element.252, f32[128,128,512]{1,0,2:T(8,128)} %copy.319, pred[128,128]{1,0:T(8,128)(4,1)S(1)} %copy-done.60, pred[128,128]{1,0:T(8,128)(4,1)S(1)} %copy-done.67, f32[2,8,128,512]{2,1,0,3:T(8,128)} %copy.331), kind=kOutput, calls=%fused_computation.74 | convolution fusion | flops 1628438528 | bytes 46170112 | tf_op jit(solution)/shard_map/transpose(jvp(jts,bcsj->bctj))/dot_general | solution.py:47
  1036.2 6.1 fusion.26
  1042.4 6.2 fusion.29
  1053.1 41.6 %all-reduce.5 = (f32[2,512]{1,0:T(2,128)S(1)}, f32[4,128]{1,0:T(4,128)S(1)}) all-reduce(f32[2,512]{1,0:T(2,128)S(1)} %pad_maximum_fusion, f32[4,128]{1,0:T(4,128)S(1)} %pad_maximum_fusion.1), channel_id=1, replica_groups=mesh['dp'=8,'fsdp'=4] {'dp','fsdp'}, use_global_device_ids=true, to_apply=%region_14.15 | all-reduce | flops 1536 | bytes 12288 | tf_op jit(solution)/shard_map/psum | solution.py:284
  1096.0 141.1 %all-reduce.9.cloned.1.call-done = (f32[4,512,16]{1,2,0:T(8,128)}, f32[512,128]{1,0:T(8,128)}, f32[512,1024]{1,0:T(8,128)}, f32[512,1024]{1,0:T(8,128)}, f32[512...) async-done(((f32[4,512,16]{1,2,0:T(8,128)}, f32[512,128]{1,0:T(8,128)}, f32[512,1024]{1,0:T(8,128)}, ...) | async-done | bytes 12976144 | tf_op jit(solution)/shard_map/psum | solution.py:284
  (458 shorter events, 211.7 us)
Async XLA Ops:
  7.2 13.4 %copy-start.109 = (bf16[4,32]{1,0:T(4,128)(2,1)S(1)}, bf16[4,32]{1,0:T(4,128)(2,1)}, u32[]{:S(2)}) copy-start(bf16[4,32]{1,0:T(4,128)(2,1)} %param.22) | copy-start | bytes 772
  7.2 333.8 %all-gather.9.cloned.1.call-start = ((), (), s32[]{:S(2)}) async-start(), calls=%async_computation.1 | async-start | bytes 1310720 | tf_op jit(solution)/shard_map/all_gather | solution.py:100
  7.9 347.2 %all-gather.7.cloned.1.call-start = ((), (), s32[]{:S(2)}) async-start(), calls=%async_computation | async-start | bytes 1310720 | tf_op jit(solution)/shard_map/all_gather | solution.py:101
  8.7 355.9 %all-gather.11.cloned.1.call-start = ((), (), s32[]{:S(2)}) async-start(), calls=%async_computation.2 | async-start | bytes 1310720 | tf_op jit(solution)/shard_map/all_gather | solution.py:104
  9.4 367.8 %all-gather.13.cloned.1.call-start = ((), (), s32[]{:S(2)}) async-start(), calls=%async_computation.3 | async-start | bytes 1310720 | tf_op jit(solution)/shard_map/all_gather | solution.py:105
  10.0 377.8 %all-gather.15.cloned.1.call-start = ((), (), s32[]{:S(2)}) async-start(), calls=%async_computation.4 | async-start | bytes 1310720 | tf_op jit(solution)/shard_map/all_gather | solution.py:106
  10.6 1226.5 %all-reduce.9.cloned.1.call-start = ((), (), s32[]{:S(2)}) async-start(), calls=%async_computation.5 | async-start | bytes 25952256 | tf_op jit(solution)/shard_map/psum | solution.py:284
  10.6 140.3 %copy-start.100 = (f32[128]{0:T(128)}, f32[128]{0:T(128)S(1)}, u32[]{:S(2)}) copy-start(f32[128]{0:T(128)S(1)} %iota_convert_fusion) | copy-start | bytes 1540
  17.2 133.7 %copy-start.61 = (f32[512,16]{0,1:T(8,128)}, f32[512,16]{0,1:T(8,128)S(1)}, u32[]{:S(2)}) copy-start(f32[512,16]{0,1:T(8,128)S(1)} %log_bitcast_fusion) | copy-start | bytes 98308
  17.2 13.5 %copy-start.110 = (bf16[2,128]{1,0:T(2,128)(2,1)S(1)}, bf16[2,128]{1,0:T(2,128)(2,1)}, u32[]{:S(2)}) copy-start(bf16[2,128]{1,0:T(2,128)(2,1)} %param.20) | copy-start | bytes 1540
  17.9 19.0 %copy-start.93 = (bf16[128,128]{1,0:T(8,128)(2,1)S(1)}, bf16[128,128]{1,0:T(8,128)(2,1)}, u32[]{:S(2)}) copy-start(bf16[128,128]{1,0:T(8,128)(2,1)} %param.23) | copy-start | bytes 98308
  19.8 26.1 %copy-start.68 = (f32[512,16]{0,1:T(8,128)}, f32[512,16]{0,1:T(8,128)S(1)}, u32[]{:S(2)}) copy-start(f32[512,16]{0,1:T(8,128)S(1)} %get-tuple-element.607) | copy-start | bytes 98308
  19.8 26.1 %copy-start.70 = (f32[512,16]{0,1:T(8,128)}, f32[512,16]{0,1:T(8,128)S(1)}, u32[]{:S(2)}) copy-start(f32[512,16]{0,1:T(8,128)S(1)} %get-tuple-element.609) | copy-start | bytes 98308
  19.8 37.8 %copy-start.72 = (f32[512,16]{0,1:T(8,128)}, f32[512,16]{0,1:T(8,128)S(1)}, u32[]{:S(2)}) copy-start(f32[512,16]{0,1:T(8,128)S(1)} %get-tuple-element.606) | copy-start | bytes 98308
  20.5 130.4 %copy-start.76 = (f32[512,16]{0,1:T(8,128)}, f32[512,16]{0,1:T(8,128)S(1)}, u32[]{:S(2)}) copy-start(f32[512,16]{0,1:T(8,128)S(1)} %get-tuple-element.605) | copy-start | bytes 98308
  20.6 259.6 %copy-start.59 = (pred[128,128]{1,0:T(8,128)(4,1)}, pred[128,128]{1,0:T(8,128)(4,1)S(1)}, u32[]{:S(2)}) copy-start(pred[128,128]{1,0:T(8,128)(4,1)S(1)} %get-tuple-element.633) | copy-start | bytes 49156
  20.6 259.6 %copy-start.66 = (pred[128,128]{1,0:T(8,128)(4,1)}, pred[128,128]{1,0:T(8,128)(4,1)S(1)}, u32[]{:S(2)}) copy-start(pred[128,128]{1,0:T(8,128)(4,1)S(1)} %get-tuple-element.632) | copy-start | bytes 49156
  30.7 21.2 %copy-start.7 = (bf16[2048,512]{0,1:T(8,128)(2,1)}, bf16[2048,512]{0,1:T(8,128)(2,1)S(1)}, u32[]{:S(2)}) copy-start(bf16[2048,512]{0,1:T(8,128)(2,1)S(1)} %copy.318) | copy-start | bytes 6291460
  36.3 15.5 %copy-start.96 = (f32[1,512]{1,0:T(1,128)}, f32[1,512]{1,0:T(1,128)S(1)}, u32[]{:S(2)}) copy-start(f32[1,512]{1,0:T(1,128)S(1)} %get-tuple-element.613) | copy-start | bytes 6148
  36.8 15.0 %copy-start.91 = (f32[2048]{0:T(1024)}, f32[2048]{0:T(1024)S(1)}, u32[]{:S(2)}) copy-start(f32[2048]{0:T(1024)S(1)} %fusion.30) | copy-start | bytes 24580
  36.8 15.1 %copy-start.85 = (f32[2048]{0:T(1024)}, f32[2048]{0:T(1024)S(1)}, u32[]{:S(2)}) copy-start(f32[2048]{0:T(1024)S(1)} %fusion.125) | copy-start | bytes 24580
  216.4 35.7 %copy-start.108 = (s32[2]{0:T(128)S(1)}, s32[2]{0:T(128)}, u32[]{:S(2)}) copy-start(s32[2]{0:T(128)} %param.19) | copy-start | bytes 28
  216.4 35.9 %copy-start.80 = (bf16[128,512]{1,0:T(8,128)(2,1)S(1)}, bf16[128,512]{1,0:T(8,128)(2,1)}, u32[]{:S(2)}) copy-start(bf16[128,512]{1,0:T(8,128)(2,1)} %param.27) | copy-start | bytes 393220
  216.4 44.1 %copy-start.81 = (bf16[128,512]{1,0:T(8,128)(2,1)S(1)}, bf16[128,512]{1,0:T(8,128)(2,1)}, u32[]{:S(2)}) copy-start(bf16[128,512]{1,0:T(8,128)(2,1)} %param.26) | copy-start | bytes 393220
  216.4 51.8 %copy-start.39 = (bf16[2048,512]{1,0:T(8,128)(2,1)S(1)}, bf16[2048,512]{1,0:T(8,128)(2,1)}, u32[]{:S(2)}) copy-start(bf16[2048,512]{1,0:T(8,128)(2,1)} %param.31) | copy-start | bytes 6291460
  270.7 9.5 copy-start.5
  280.2 56.0 %copy-start.64 = (bf16[512,128]{1,0:T(8,128)(2,1)S(1)}, bf16[512,128]{1,0:T(8,128)(2,1)}, u32[]{:S(2)}) copy-start(bf16[512,128]{1,0:T(8,128)(2,1)} %all_gather.47) | copy-start | bytes 393220
  280.2 56.0 %copy-start.111 = (f32[128]{0:T(128)S(1)}, f32[128]{0:T(128)}, u32[]{:S(2)}) copy-start(f32[128]{0:T(128)} %get-tuple-element.614) | copy-start | bytes 1540
  280.2 56.0 %copy-start.112 = (f32[128]{0:T(128)S(1)}, f32[128]{0:T(128)}, u32[]{:S(2)}) copy-start(f32[128]{0:T(128)} %get-tuple-element.615) | copy-start | bytes 1540
  280.2 56.0 %copy-start.113 = (f32[128]{0:T(128)S(1)}, f32[128]{0:T(128)}, u32[]{:S(2)}) copy-start(f32[128]{0:T(128)} %get-tuple-element.616) | copy-start | bytes 1540
  280.3 56.0 %copy-start.114 = (f32[128]{0:T(128)S(1)}, f32[128]{0:T(128)}, u32[]{:S(2)}) copy-start(f32[128]{0:T(128)} %get-tuple-element.617) | copy-start | bytes 1540
  377.1 158.7 %copy-start.89 = (f32[2048]{0:T(1024)}, f32[2048]{0:T(1024)S(1)}, u32[]{:S(2)}) copy-start(f32[2048]{0:T(1024)S(1)} %fusion.126) | copy-start | bytes 24580
  387.8 8.6 copy-start.21
  387.8 8.6 copy-start.118
  400.0 7.8 copy-start.26
  400.0 7.8 copy-start.83
  407.9 25.3 %copy-start.37 = (bf16[2048,512]{0,1:T(8,128)(2,1)}, bf16[2048,512]{0,1:T(8,128)(2,1)S(1)}, u32[]{:S(2)}) copy-start(bf16[2048,512]{0,1:T(8,128)(2,1)S(1)} %get-tuple-element.591) | copy-start | bytes 6291460
  442.9 12.3 copy-start.3
  442.9 12.3 copy-start.12
  455.2 10.1 copy-start.6
  455.2 10.1 copy-start.60
  465.3 57.0 %copy-start.17 = (bf16[2,8,128,512]{2,1,0,3:T(8,128)(2,1)S(1)}, bf16[2,8,128,512]{2,1,0,3:T(8,128)(2,1)}, u32[]{:S(2)}) copy-start(bf16[2,8,128,512]{2,1,0,3:T(8,128)(2,1)} %copy-done.15) | copy-start | bytes 6291460
  465.3 57.0 %copy-start.53 = (bf16[2048,128]{1,0:T(8,128)(2,1)S(1)}, bf16[2048,128]{1,0:T(8,128)(2,1)}, u32[]{:S(2)}) copy-start(bf16[2048,128]{1,0:T(8,128)(2,1)} %copy-done.52) | copy-start | bytes 1572868
  465.3 58.4 %copy-start.122 = (bf16[2048,1024]{1,0:T(8,128)(2,1)S(1)}, bf16[2048,1024]{1,0:T(8,128)(2,1)}, u32[]{:S(2)}) copy-start(bf16[2048,1024]{1,0:T(8,128)(2,1)} %get-tuple-element.594) | copy-start | bytes 12582916
  548.7 8.1 copy-start
  581.6 8.1 copy-start
  614.6 8.1 copy-start
  647.6 8.1 copy-start
  680.5 8.1 copy-start
  713.5 8.1 copy-start
  746.5 8.1 copy-start
  779.5 8.1 copy-start
  852.2 112.6 %copy-start.62 = (f32[512,16]{0,1:T(8,128)S(1)}, f32[512,16]{0,1:T(8,128)}, u32[]{:S(2)}) copy-start(f32[512,16]{0,1:T(8,128)} %copy-done.61) | copy-start | bytes 98308
  852.2 112.6 %copy-start.101 = (f32[128]{0:T(128)S(1)}, f32[128]{0:T(128)}, u32[]{:S(2)}) copy-start(f32[128]{0:T(128)} %copy-done.100) | copy-start | bytes 1540
  965.6 7.5 copy-start.9
  973.1 8.8 copy-start.63
  973.1 8.8 copy-start.69
  973.2 8.8 copy-start.71
  973.2 8.8 copy-start.77
  973.2 8.8 copy-start.78
  1002.2 33.8 %copy-start.44 = (bf16[2048,1024]{1,0:T(8,128)(2,1)S(1)}, bf16[2048,1024]{1,0:T(8,128)(2,1)}, u32[]{:S(2)}) copy-start(bf16[2048,1024]{1,0:T(8,128)(2,1)} %copy-done.43) | copy-start | bytes 12582916
  1002.2 33.8 %copy-start.88 = (f32[2048]{0:T(1024)S(1)}, f32[2048]{0:T(1024)}, u32[]{:S(2)}) copy-start(f32[2048]{0:T(1024)} %copy-done.85) | copy-start | bytes 24580
  1002.2 33.8 %copy-start.99 = (f32[1,512]{1,0:T(1,128)S(1)}, f32[1,512]{1,0:T(1,128)}, u32[]{:S(2)}) copy-start(f32[1,512]{1,0:T(1,128)} %copy-done.96) | copy-start | bytes 6148
  1002.2 33.8 %copy-start.115 = (bf16[512,1024]{1,0:T(8,128)(2,1)S(1)}, bf16[512,1024]{1,0:T(8,128)(2,1)}, u32[]{:S(2)}) copy-start(bf16[512,1024]{1,0:T(8,128)(2,1)} %all-gather.9.cloned.1.call-done) | copy-start | bytes 3145732
  (87 other events, 335.5 us)
Sparse Core Ops, SparseCore 0:
  9.6 19.4 all-gather.8
  30.6 17.4 all-gather.6
  49.6 16.7 all-gather.10
  67.8 16.7 all-gather.12
  86.0 16.7 all-gather.14
  986.7 250.3 all-reduce.8
where the time goes:
time: 1270 us; the launch traced here: 1260 us
  matrix products  472 us (37%)
  local copies, waits for them, and re-layouts  376 us (30%)
  other arithmetic  169 us (13%)
  waiting for transfers between devices  144 us (11%)
  blocking collectives  80.7 us (6%)
  between operations  15.8 us (1%)
    dot_general x24, matrix products, advance(): jnp.einsum('sjh,bsj->bjh', absorb_table, block_in, precision=highest)  170 us
    dot_general x3, matrix products, smooth(): jnp.einsum('jts,bcsj->bctj', toeplitz, pieces, precision=highest)  147 us
    psum x1, waiting for transfers between devices, per_device(): lax.psum((totals[0], totals[1], totals[2], totals[3], totals[4], totals[5...  141 us
    dynamic_update_slice x8, local copies, waits for them, and re-layouts, smooth(): unused, states = lax.scan(jax.checkpoint(advance), initial, ordered)  116 us
    scatter-add x1, other arithmetic, smooth(): jnp.take(kernel, jnp.maximum(lag_table, 0), axis=1)  104 us
    gather x2, local copies, waits for them, and re-layouts, smooth(): jnp.take(kernel, jnp.maximum(lag_table, 0), axis=1)  100 us
    dot_general x8, matrix products, matmul(): return jnp.dot(left, right, preferred_element_type=jnp.float32)  50 us
    psum x1, blocking collectives, per_device(): lax.psum((totals[0], totals[1], totals[2], totals[3], totals[4], totals[5...  41.6 us
  transfers between devices with their start and end apart: 6, of which 1 were waited for; matrix products, arithmetic and copies ran while one was open for 32% of the time, Pallas kernels for 0%

commit v1 on v0

v1 whole, which is shorter than its diff:
```python
import functools

import jax
import jax.numpy as jnp
import numpy as np
from jax import lax
from jax.experimental import pallas as pl
from jax.experimental.pallas import tpu as pltpu
from jax.sharding import PartitionSpec as P

bf = jnp.bfloat16
f32 = jnp.float32
SPAN = 128
CH = 256
NH = 16
LG = 128
eps = 1e-6


def dft_tables():
    f=np.arange(CH)[:,None]+0.5
    m=np.arange(-CH,CH)[None,:]
    ang=2*np.pi*f*m/(2*CH)
    both=np.concatenate([np.cos(ang),np.sin(ang)],axis=0)
    return both.astype(np.float32)

def mm(a,b): return jnp.dot(a,b,preferred_element_type=f32)
def mm_tn(a,b): return lax.dot_general(a,b,(((0,),(0,)),((),())),preferred_element_type=f32)
def mm_nt(a,b): return lax.dot_general(a,b,(((1,),(1,)),((),())),preferred_element_type=f32)

def ema_rates(p):
    a=jax.nn.sigmoid(p[0]); g=jax.nn.sigmoid(p[1])
    return a,g,p[2],p[3],1.0-a*g

def power_of(base, n):
    out=None
    sq=base
    while n:
        if n&1: out = sq if out is None else out*sq
        n>>=1
        if n: sq=sq*sq
    return out

def ladder(keep, width):
    r=lax.broadcasted_iota(jnp.int32,(width,keep.shape[-1]),0)
    acc=jnp.ones((width,keep.shape[-1]),f32)
    sq=keep
    bit=1
    while bit<width:
        acc=acc*jnp.where((r&bit)!=0, sq, 1.0)
        sq=sq*sq
        bit*=2
    return acc

MESH = pl.DeviceIdType.MESH


def flip(i, bit):
    return i + bit - 2 * bit * ((i // bit) % 2)


def const_spec(a):
    nd = len(a.shape)
    return pl.BlockSpec(a.shape, lambda i: (0,) * nd, pipeline_mode=pl.Buffered(1))


ANY = pl.BlockSpec(memory_space=pl.ANY)


class Gather:
    def __init__(self, shards, outs, pieces, send, recv, local):
        self.shards, self.outs, self.pieces = shards, outs, pieces
        self.send, self.recv, self.local = send, recv, local
        self.dp = lax.axis_index("dp")
        self.fs = lax.axis_index("fsdp")
        self.x = self.dp % 2
        self.core_peer = (self.dp, flip(self.fs, 1))
        self.y_peer = (self.dp, flip(self.fs, 2))
        self.x_peer = (flip(self.dp, 1), self.fs)

    def peers(self):
        return [self.core_peer, self.y_peer, self.x_peer]

    def copy(self, p, k):
        a, first, r = self.pieces[p]
        shard, out = self.shards[a], self.outs[a]
        n = shard.shape[0]
        h = n // 2
        half = self.x * h + first
        other = (1 - self.x) * h + first
        far = flip(self.fs, 2) * n
        at = lambda ref, row: ref.at[pl.ds(pl.multiple_of(row, r), r)]
        src, dst, peer = (
            (at(shard, half), at(out, self.fs * n + half), self.y_peer),
            (at(out, far + half), at(out, far + half), self.x_peer),
            (at(out, far + half), at(out, far + half), self.core_peer),
            (at(out, far + other), at(out, far + other), self.core_peer),
        )[k]
        return pltpu.make_async_remote_copy(
            src_ref=src, dst_ref=dst, send_sem=self.send.at[4 * p + k], recv_sem=self.recv.at[4 * p + k],
            device_id=peer, device_id_type=MESH)

    def whole(self, a):
        n = self.shards[a].shape[0]
        slot = 4 * len(self.pieces) + a
        return pltpu.make_async_remote_copy(
            src_ref=self.shards[a], dst_ref=self.outs[a].at[pl.ds(pl.multiple_of(self.fs * n, n), n)],
            send_sem=self.send.at[slot], recv_sem=self.recv.at[slot], device_id=self.core_peer, device_id_type=MESH)

    def own(self, a):
        n = self.shards[a].shape[0]
        mine = pl.ds(pl.multiple_of(self.fs * n, n), n)
        return pltpu.make_async_copy(self.shards[a], self.outs[a].at[mine], self.local.at[a])

    def begin(self):
        for p in range(len(self.pieces)):
            self.copy(p, 0).start()
        for a in range(len(self.shards)):
            self.whole(a).start()
            self.own(a).start()

    def relay(self, p):
        self.copy(p, 0).wait_recv()
        self.copy(p, 1).start()
        self.copy(p, 2).start()

    def last(self, p):
        self.copy(p, 1).wait_recv()
        self.copy(p, 3).start()

    def finish(self):
        for p in range(len(self.pieces)):
            for k in range(4):
                self.copy(p, k).wait_send()
            for k in (2, 3):
                self.copy(p, k).wait_recv()
        for a in range(len(self.shards)):
            self.whole(a).wait()
            self.own(a).wait()


def gather_sems(arrays, pieces):
    sem = pltpu.SemaphoreType.DMA((4 * pieces + arrays,))
    return [sem, sem, pltpu.SemaphoreType.DMA((arrays,))]


SMALL = 4 * NH + 8
PIECES = ((0, 0, 32), (0, 32, 32), (1, 0, 128))


def ema_fwd_kernel(nseq, seqlen, remote, tok, dft, *rest):
    rest = list(rest)

    def take(n):
        out = rest[:n]
        del rest[:n]
        return out

    g = pl.program_id(0)
    nch = seqlen // CH
    rows = nseq * seqlen
    if remote:
        ema_i, gain_i, aff_i, *parts = take(9)
    else:
        small, = take(1)
    normed_o, smooth_o, xs_o, ks_o = take(4)
    if remote:
        small_o, aff_o, w_full, u_full = take(4)
    nscr, kscr, kspec, xspec, yspec = take(5)
    if remote:
        small, own, s1, r1, *sems = take(7)
        fs = lax.axis_index("fsdp")
        gather = Gather((own, parts[5]), (w_full, u_full), PIECES, *sems)
        across = [pltpu.make_async_remote_copy(
            src_ref=small.at[fs], dst_ref=small.at[fs], send_sem=s1.at[k], recv_sem=r1.at[k],
            device_id=peer, device_id_type=MESH) for k, peer in enumerate(fsdp_peers())]

    def slot(at, fn):
        if remote:
            pl.when(g == at)(fn)

    def open_up():
        greet(fsdp_peers() + [gather.x_peer])
        for i in range(4):
            small[fs, i * NH:(i + 1) * NH, :] = ema_i[i].astype(f32)
        tail = [gain_i[...].astype(f32), jnp.concatenate([aff_i[...].astype(f32)] * 4, axis=1),
                jnp.zeros((2, LG), f32)]
        small[fs, 4 * NH:, :] = jnp.concatenate(tail, axis=0)
        at = 0
        for w in parts[:5]:
            own[:, at:at + w.shape[1]] = w[...]
            at += w.shape[1]
        met(4)
        for c in across:
            c.start()
        gather.begin()

    slot(0, open_up)

    @pl.when(g == 0)
    def _():
        def body(i, _):
            r = pl.ds(pl.multiple_of(i * 256, 256), 256)
            x = tok[r, :].astype(f32)
            n = x * lax.rsqrt(jnp.mean(x * x, axis=-1, keepdims=True) + eps)
            for q in range(x.shape[1] // LG):
                nscr[q, r, :] = n[:, q * LG:(q + 1) * LG]
            return 0
        lax.fori_loop(0, rows // 256, body, 0)

    def settle():
        for c in across:
            c.wait()
        small_o[...] = small[...]
        for q in range(4):
            n = aff_i.shape[1]
            aff_o[:, q * n:(q + 1) * n] = small[q, 4 * NH + 2:4 * NH + 6, 0:n]

    slot(0, settle)
    slot(1, lambda: gather.relay(0))
    slot(2, lambda: gather.relay(1))
    slot(3, lambda: gather.relay(2))
    p = [small[g, i * NH:(i + 1) * NH, :] for i in range(4)]
    normed = (nscr[g] * small[g, 4 * NH:4 * NH + 1, :]).astype(bf)
    normed_o[...] = normed
    a, gg, ex, ro, keep = ema_rates(p)
    w = a * ex * ro * (1.0 / CH)
    step = power_of(keep, 16)
    z0 = []
    st = []
    for h in range(NH):
        z0.append(ladder(keep[h:h + 1, :], 16) * w[h:h + 1, :])
        st.append(jnp.broadcast_to(step[h:h + 1, :], (8, LG)))

    def kgen(i, zs):
        acc = zs[0]
        for h in range(1, NH):
            acc = acc + zs[h]
        kscr[pl.ds(pl.multiple_of(CH + i * 16, 16), 16), :] = acc.astype(bf)
        return tuple(jnp.concatenate([zs[h][:8] * st[h], zs[h][8:] * st[h]], axis=0) for h in range(NH))

    lax.fori_loop(0, seqlen // 16, kgen, tuple(z0), unroll=2)
    kscr[0:CH, :] = jnp.zeros((CH, LG), bf)
    for d in range(nch):
        kd = mm(dft[...], kscr[d * CH:(d + 2) * CH, :])
        kspec[d] = kd
        ks_o[d] = kd.astype(bf)
    fwd = dft[:, CH:]
    for c in range(nseq * nch):
        xd = mm(fwd, normed[c * CH:(c + 1) * CH, :])
        xspec[c] = xd
        xs_o[c] = xd.astype(bf)

    slot(2, lambda: gather.last(0))
    slot(3, lambda: gather.last(1))

    def point(i, _):
        rc = pl.ds(pl.multiple_of(i * 16, 16), 16)
        rs = pl.ds(pl.multiple_of(CH + i * 16, 16), 16)
        kc = [kspec[d, rc, :] for d in range(nch)]
        ks = [kspec[d, rs, :] for d in range(nch)]
        for b in range(nseq):
            xc = [xspec[b * nch + c, rc, :] for c in range(nch)]
            xs = [xspec[b * nch + c, rs, :] for c in range(nch)]
            for c in range(nch):
                yc = 0.
                ys = 0.
                for d in range(c + 1):
                    yc = yc + kc[d] * xc[c - d] - ks[d] * xs[c - d]
                    ys = ys + kc[d] * xs[c - d] + ks[d] * xc[c - d]
                yspec[b * nch + c, rc, :] = yc.astype(bf)
                yspec[b * nch + c, rs, :] = ys.astype(bf)
        return 0

    lax.fori_loop(0, CH // 16, point, 0)
    for c in range(nseq * nch):
        smooth_o[c * CH:(c + 1) * CH, :] = mm_tn(fwd, yspec[c]).astype(bf)

    def close():
        gather.last(2)
        gather.finish()

    slot(3, close)


def ema_forward(tokens, dft, nseq, small=None, comm_in=None):
    rows, D = tokens.shape
    seqlen = rows // nseq
    nch = seqlen // CH
    ng = D // LG
    nchunks = nseq * nch
    remote = comm_in is not None
    col = pl.BlockSpec((rows, LG), lambda g: (0, g))
    ins = [tokens, dft] + (list(comm_in) if remote else [small])
    wide = jax.ShapeDtypeStruct((rows, D), bf)
    outs = [(wide, col), (wide, col),
            (jax.ShapeDtypeStruct((nchunks, 2 * CH, D), bf), pl.BlockSpec((nchunks, 2 * CH, LG), lambda g: (0, 0, g))),
            (jax.ShapeDtypeStruct((nch, 2 * CH, D), bf), pl.BlockSpec((nch, 2 * CH, LG), lambda g: (0, 0, g)))]
    scratch = [pltpu.VMEM((ng, rows, LG), f32), pltpu.VMEM((seqlen + CH, LG), bf), pltpu.VMEM((nch, 2 * CH, LG), f32),
               pltpu.VMEM((nchunks, 2 * CH, LG), f32), pltpu.VMEM((nchunks, 2 * CH, LG), bf)]
    params = {}
    if remote:
        n = sum(w.shape[1] for w in comm_in[3:8])
        u = comm_in[8]
        a = jax.ShapeDtypeStruct((4, SMALL, LG), f32)
        b = jax.ShapeDtypeStruct((4, 4 * comm_in[2].shape[1]), f32)
        outs += [(a, const_spec(a)), (b, const_spec(b)), (jax.ShapeDtypeStruct((D, n), bf), ANY),
                 (jax.ShapeDtypeStruct((4 * u.shape[0], D), bf), ANY)]
        sem = pltpu.SemaphoreType.DMA((3,))
        scratch += [pltpu.VMEM(a.shape, f32), pltpu.VMEM((D // 4, n), bf), sem, sem] + gather_sems(2, len(PIECES))
        params = dict(collective_id=1, has_side_effects=True)
    return pl.pallas_call(
        functools.partial(ema_fwd_kernel, nseq, seqlen, remote),
        grid=(ng,),
        in_specs=[const_spec(a) for a in ins],
        out_specs=[o[1] for o in outs],
        out_shape=[o[0] for o in outs],
        scratch_shapes=scratch,
        compiler_params=pltpu.CompilerParams(vmem_limit_bytes=60 * 2**20, **params),
        name="ema_fwd",
    )(*ins)


class Reduce:
    def __init__(self, q, send, recv, **refs):
        self.q, self.send, self.recv = q, send, recv
        self.__dict__.update(refs)
        self.dp = lax.axis_index("dp")
        self.fs = lax.axis_index("fsdp")
        self.x = self.dp % 2
        self.z = self.dp // 2
        self.y = self.fs // 2

    def rows(self, at, count):
        return pl.ds(pl.multiple_of(at, self.q), count)

    def remote(self, src, dst, slot, device):
        return pltpu.make_async_remote_copy(
            src_ref=src, dst_ref=dst, send_sem=self.send.at[slot], recv_sem=self.recv.at[slot],
            device_id=device, device_id_type=MESH)

    def line(self):
        for i, oz in enumerate((3, 2, 1)):
            dp = self.dp
            if oz & 1:
                dp = flip(dp, 2)
            if oz & 2:
                dp = flip(dp, 4)
            yield i, dp

    def copies(self, stage):
        q = self.q
        if stage == "core":
            return [self.remote(self.give, self.core_in, 0, (self.dp, flip(self.fs, 1)))]
        if stage == "y":
            return [self.remote(self.core_in.at[1 - self.y], self.y_in, 1, (self.dp, flip(self.fs, 2)))]
        if stage == "x":
            return [self.remote(self.y_in.at[self.rows((1 - self.x) * 4 * q, 4 * q)], self.x_in, 2,
                                (flip(self.dp, 1), self.fs))]
        if stage == "z":
            return [self.remote(self.x_in.at[self.rows((dp // 2) * q, q)], self.z_in.at[i], 3 + i, (dp, self.fs))
                    for i, dp in self.line()]
        if stage == "back_z":
            mine = self.full.at[self.own_piece()]
            return [self.remote(mine, mine, 6 + i, (dp, self.fs)) for i, dp in self.line()]
        half = self.full.at[self.rows(self.x * 4 * q, 4 * q)]
        return [self.remote(half, half, 9, (flip(self.dp, 1), self.fs))]

    def start(self, stage):
        for c in self.copies(stage):
            c.start()

    def wait(self, stage):
        for c in self.copies(stage):
            c.wait()

    def add_core(self):
        self.wait("core")
        step = 2 * self.q
        for y in range(2):
            @pl.loop(0, 4)
            def _(i):
                r = pl.ds(pl.multiple_of(i * step, step), step)
                self.core_in[y, r, :] = (self.core_in[y, r, :].astype(f32) + self.keep[y, r, :].astype(f32)).astype(bf)

    def add_y(self):
        self.wait("y")
        step = 2 * self.q

        @pl.loop(0, 4)
        def _(i):
            r = pl.ds(pl.multiple_of(i * step, step), step)
            self.y_in[r, :] = (self.y_in[r, :].astype(f32) + self.core_in[self.y, r, :].astype(f32)).astype(bf)

    def add_x(self):
        self.wait("x")
        q = self.q

        @pl.loop(0, 4)
        def _(i):
            r = self.rows(i * q, q)
            k = self.rows((self.x * 4 + i) * q, q)
            self.x_in[r, :] = (self.x_in[r, :].astype(f32) + self.y_in[k, :].astype(f32)).astype(bf)

    def add_z(self):
        self.wait("z")
        q = self.q
        total = self.x_in[self.rows(self.z * q, q), :].astype(f32)
        for i in range(3):
            total += self.z_in[i].astype(f32)
        return total.astype(bf)

    def own_piece(self):
        return self.rows((self.x * 4 + self.z) * self.q, self.q)


def greet(peers):
    sem = pltpu.get_barrier_semaphore()
    for peer in peers:
        pl.semaphore_signal(sem, inc=1, device_id=peer, device_id_type=MESH)


def met(count):
    pl.semaphore_wait(pltpu.get_barrier_semaphore(), count)


def dp_peers():
    dp, fs = lax.axis_index("dp"), lax.axis_index("fsdp")
    out = []
    for k in range(1, 8):
        d = dp
        for bit in (1, 2, 4):
            if k & bit:
                d = flip(d, bit)
        out.append((d, fs))
    return out


def fsdp_peers():
    dp, fs = lax.axis_index("dp"), lax.axis_index("fsdp")
    return [(dp, flip(fs, 1)), (dp, flip(fs, 2)), (dp, flip(flip(fs, 1), 2))]


def blocks(accs, shard):
    at = 0
    for acc in accs:
        n = acc.shape[0] // 4
        rows = pl.ds(pl.multiple_of(shard * n, n), n)
        for j in range(acc.shape[1] // LG):
            yield at, n, acc[rows, j * LG:(j + 1) * LG]
            at += n


def pack(accs, dst, core):
    for y in range(2):
        for at, n, block in blocks(accs, 2 * y + core):
            dst[y, at:at + n, :] = block.astype(bf)


def pack_add(accs, dst, core):
    for y in range(2):
        for at, n, block in blocks(accs, 2 * y + core):
            dst[y, at:at + n, :] = (block + dst[y, at:at + n, :].astype(f32)).astype(bf)


def unpack(full, outs):
    at = 0
    for out in outs:
        n = out.shape[0]
        for j in range(out.shape[1] // LG):
            out[:, j * LG:(j + 1) * LG] = full[at:at + n, :].astype(f32)
            at += n


RT = 512


def sigm(v):
    return 0.5 * jnp.tanh(0.5 * v) + 0.5


def tile_valid(lens, step, seqlen):
    row0 = step * RT
    seq = row0 // seqlen
    return row0 - seq * seqlen, lens[seq]


def split_pack(w_a):
    zd = SPAN
    d = w_a.shape[0]
    vd = (w_a.shape[1] - zd - 2 * d) // 2
    cuts = [0, zd, zd + vd, zd + vd + d, zd + vd + 2 * d, zd + 2 * vd + 2 * d]
    return [w_a.at[:, lo:hi] for lo, hi in zip(cuts, cuts[1:])]


def forward_kernel(seqlen, remote, lens, sm, nm, tok, aff, w_a, u_h, *rest):
    shards, rest = (rest[:2], rest[2:]) if remote else ((), rest)
    middle_o, upd_o, u2_o, uh_o, val_o, vsl_o, gat_o, rv_o, a2_o, pr_o, qk_o = rest[:11]
    rest = rest[11:]
    if remote:
        gather = Gather(shards, rest[:2], ((0, 0, 64), (1, 0, 128)), *rest[3:])
        rest = rest[2:]
    gscr = rest[0]

    def slot(at, fn):
        if remote:
            pl.when(pl.program_id(0) == at)(fn)

    slot(0, lambda: greet(gather.peers()))

    w_z, w_r, w_u, w_h, w_v = split_pack(w_a)
    base, length = tile_valid(lens, pl.program_id(0), seqlen)
    zd = w_z.shape[1]
    vd = w_v.shape[1]
    s = sm[...]
    n = nm[...]
    scale = zd ** -0.5
    zp = mm(s, w_z[...])
    sg = sigm(zp)
    sh = zp * sg
    ssl = sg + sh * (1.0 - sg)
    q = (sh * aff[0:1, :] + aff[1:2, :]).astype(bf)
    k = (sh * aff[2:3, :] + aff[3:4, :]).astype(bf)
    qk_o[0] = q
    qk_o[1] = k
    qk_o[2] = sh.astype(bf)
    qk_o[3] = ssl.astype(bf)
    probs = []
    for b in range(RT // SPAN):
        r = slice(b * SPAN, (b + 1) * SPAN)
        sc = mm_nt(q[r], k[r]) * scale
        keys = base + b * SPAN + lax.broadcasted_iota(jnp.int32, (1, SPAN), 1)
        sc = jnp.where(keys < length, sc, -1e9)
        e = jnp.exp(sc - jnp.max(sc, axis=-1, keepdims=True))
        p = (e / jnp.sum(e, axis=-1, keepdims=True)).astype(bf)
        pr_o[r, :] = p
        probs.append(p)
    rows = base + lax.broadcasted_iota(jnp.int32, (RT, 1), 0)
    live = (rows < length).astype(f32)
    for j in range(vd // 256):
        c = slice(j * 256, (j + 1) * 256)
        vp = mm(n, w_v[:, c])
        sg = sigm(vp)
        v = vp * sg
        vl = v.astype(bf)
        val_o[:, c] = vl
        vsl_o[:, c] = (sg + v - v * sg).astype(bf)
        att = jnp.concatenate(
            [mm(probs[b], vl[b * SPAN:(b + 1) * SPAN]) for b in range(RT // SPAN)], axis=0)
        rp = mm(s, w_r[:, c])
        sg = sigm(rp)
        re = rp * sg
        att = att * live
        ga = (re * att).astype(bf)
        gat_o[:, c] = ga
        gscr[:, c] = ga
        rv_o[:, c] = (re * live).astype(bf)
        a2_o[:, c] = (att * (sg + re - re * sg)).astype(bf)
    for j in range(w_h.shape[1] // 256):
        c = slice(j * 256, (j + 1) * 256)
        hp = mm(s, w_h[:, c]) + mm(gscr[...], u_h[:, c])
        up = sigm(mm(s, w_u[:, c]))
        x = tok[:, c].astype(f32)
        sg = sigm(hp)
        cand = hp * sg
        diff = cand - x
        ud = up * diff
        middle_o[:, c] = (x + ud).astype(bf)
        upd_o[:, c] = up.astype(bf)
        u2_o[:, c] = (ud - ud * up).astype(bf)
        uh_o[:, c] = (up * (sg + cand - cand * sg)).astype(bf)


    def begin():
        met(3)
        gather.begin()

    def relay():
        gather.relay(0)
        gather.relay(1)

    def last():
        gather.last(0)
        gather.last(1)

    slot(0, begin)
    slot(1, relay)
    slot(2, last)
    slot(3, lambda: gather.finish())


def row_spec(width):
    return pl.BlockSpec((RT, width), lambda i: (i, 0))


SMEM = pl.BlockSpec(memory_space=pltpu.SMEM)


def forward_main(lengths, smooth, normed, tokens, affine, w_a, u_h, shards=()):
    rows, D = tokens.shape
    nseq = lengths.shape[0]
    vd = u_h.shape[0]
    zd = affine.shape[1]
    d_out = jax.ShapeDtypeStruct((rows, D), bf)
    v_out = jax.ShapeDtypeStruct((rows, vd), bf)
    ds, vs = row_spec(D), row_spec(vd)
    ws = (affine, w_a, u_h)
    remote = len(shards) > 0
    params = dict(collective_id=4, has_side_effects=True) if remote else {}
    fulls = [jax.ShapeDtypeStruct((4 * w.shape[0], w.shape[1]), bf) for w in shards]
    return pl.pallas_call(
        functools.partial(forward_kernel, rows // nseq, remote),
        grid=(rows // RT,),
        in_specs=[SMEM, ds, ds, ds] + [const_spec(w) for w in (*ws, *shards)],
        out_specs=[ds] * 4 + [vs] * 5 + [row_spec(SPAN), pl.BlockSpec((4, RT, zd), lambda i: (0, i, 0))]
        + [ANY] * len(shards),
        out_shape=[d_out] * 4 + [v_out] * 5
        + [jax.ShapeDtypeStruct((rows, SPAN), bf), jax.ShapeDtypeStruct((4, rows, zd), bf)] + fulls,
        scratch_shapes=[pltpu.VMEM((RT, vd), bf)] + (gather_sems(2, 2) if remote else []),
        compiler_params=pltpu.CompilerParams(vmem_limit_bytes=60 * 2**20, **params),
        name="forward_main",
    )(lengths, smooth, normed, tokens, *ws, *shards)


def ffn_kernel(packed, fs, middle, cot, gain, w_in, w_out, out_o, dm_o, dg_o, *rest):
    if packed:
        keep_o, give_o, gwi, gwo, ascr, gscr = rest
    else:
        gwi, gwo, ascr, gscr = rest

    @pl.when(pl.program_id(0) == 0)
    def _():
        gwi[...] = jnp.zeros_like(gwi)
        gwo[...] = jnp.zeros_like(gwo)
        dg_o[...] = jnp.zeros_like(dg_o)

    m = middle[...].astype(f32)
    inv = lax.rsqrt(jnp.mean(m * m, axis=-1, keepdims=True) + eps)
    gn = lane_row(gain, 4 * NH + 1)
    mr = m * inv
    y = (mr * gn).astype(bf)
    cl = cot[...]
    for j in range(w_in.shape[1] // 256):
        c = slice(j * 256, (j + 1) * 256)
        pre = mm(y, w_in[:, c])
        sg = sigm(pre)
        act = pre * sg
        al = act.astype(bf)
        ascr[:, c] = al
        ga = mm_nt(cl, w_out[c, :])
        gf = (ga * (sg + act - act * sg)).astype(bf)
        gscr[:, c] = gf
        gwo[c, :] += mm_tn(al, cl)
        gwi[:, c] += mm_tn(y, gf)
    out_o[...] = (m + mm(ascr[...], w_out[...])).astype(bf)
    dy = mm_nt(gscr[...], w_in[...])
    dg_o[...] += jnp.sum((dy * mr).reshape(RT // 8, 8, m.shape[1]), axis=0)
    dyg = dy * gn
    inner = jnp.mean(dyg * mr, axis=-1, keepdims=True)
    dm_o[...] = (cl.astype(f32) + inv * (dyg - mr * inner)).astype(bf)
    if packed:
        @pl.when(pl.program_id(0) == pl.num_programs(0) - 1)
        def _():
            core = fs[0] % 2
            pack((gwi, gwo), give_o, 1 - core)
            pack((gwi, gwo), keep_o, core)


def ffn_main(fs, middle, cot, gains, w_in, w_out, packed):
    rows, D = middle.shape
    ff = w_in.shape[1]
    ds = row_spec(D)
    accs = [(D, ff), (ff, D)]
    pair = [jax.ShapeDtypeStruct((2, (D * ff + ff * D) // 4 // LG, LG), bf)] * 2
    extra = pair if packed else [jax.ShapeDtypeStruct(s, f32) for s in accs]
    gain = jax.ShapeDtypeStruct((8, D), f32)
    return pl.pallas_call(
        functools.partial(ffn_kernel, packed),
        grid=(rows // RT,),
        in_specs=[SMEM, ds, ds] + [const_spec(w) for w in (gains, w_in, w_out)],
        out_specs=[ds, ds] + [const_spec(a) for a in [gain] + extra],
        out_shape=[jax.ShapeDtypeStruct((rows, D), bf)] * 2 + [gain] + extra,
        scratch_shapes=([pltpu.VMEM(s, f32) for s in accs] if packed else [])
        + [pltpu.VMEM((RT, ff), bf), pltpu.VMEM((RT, ff), bf)],
        compiler_params=pltpu.CompilerParams(vmem_limit_bytes=60 * 2**20),
        name="ffn_main",
    )(fs, middle, cot, gains, w_in, w_out)


def backward_kernel(qs, remote, dm, upd, u2, uh, gat, rv, a2, sm, val, vsl, pr, qk, nm, aff, u_h, *rest):
    rest = list(rest)

    def take(n):
        out = rest[:n]
        del rest[:n]
        return out

    if remote:
        keep1, give1 = take(2)
    dxd_o, gh_o, gu_o, gr_o, gv_o, gsp_o, ga_o = take(7)
    if remote:
        piece1_o, sum2_o, sum3_o, keep4_o, give4_o = take(5)
    gz, gv, gr, gu, gh_w, guh = take(6)
    ascr, = take(1)
    step = pl.program_id(0)
    tiles = pl.num_programs(0) // 2
    if remote:
        core1, y1, x1, z1, s1, r1 = take(6)
        give2, core2, y2, s2, r2 = take(5)
        give3, core3, s3, r3 = take(4)
        one = Reduce(qs[0], s1, r1, keep=keep1, give=give1, core_in=core1, y_in=y1, x_in=x1, z_in=z1)
        two = Reduce(qs[1], s2, r2, give=give2, core_in=core2, y_in=y2)
        three = Reduce(qs[2], s3, r3, give=give3, core_in=core3)
        core = lax.axis_index("fsdp") % 2

    def slot(at, fn):
        if remote:
            pl.when(step == at)(fn)

    @pl.when(step == 0)
    def _():
        for o in (gz, gv, gr, gu, gh_w, guh, ga_o):
            o[...] = jnp.zeros_like(o)

    def open_up():
        greet(fsdp_peers() + dp_peers())
        met(10)
        one.start("core")

    slot(0, open_up)

    def first():
        one.add_core()
        one.start("y")

    slot(1, first)

    def second():
        pack((gh_w, guh, gu), give2, 1 - core)
        two.start("core")
        one.add_y()
        one.start("x")

    slot(tiles, second)

    def third():
        two.wait("core")
        pack_add((gh_w, guh, gu), core2, core)
        two.start("y")
        pack((gr,), give3, 1 - core)
        three.start("core")

    slot(tiles + 1, third)

    def fourth():
        one.add_x()
        one.start("z")

    slot(tiles + 3, fourth)

    @pl.when(step < tiles)
    def _():
        vd = u_h.shape[0]
        d = dm[...].astype(f32)
        gh = (d * uh[...].astype(f32)).astype(bf)
        gu_l = (d * u2[...].astype(f32)).astype(bf)
        gh_o[...] = gh
        gu_o[...] = gu_l
        dxd_o[...] = (d - d * upd[...].astype(f32)).astype(bf)
        s = sm[...]
        gh_w[...] += mm_tn(s, gh)
        gu[...] += mm_tn(s, gu_l)
        at = pl.ds(pl.multiple_of(step * RT, RT), RT)
        for j in range(vd // 256):
            c = slice(j * 256, (j + 1) * 256)
            dg = mm_nt(gh, u_h[c, :])
            gr_l = (dg * a2[:, c].astype(f32)).astype(bf)
            gr_o[:, c] = gr_l
            ascr[at, c] = (dg * rv[:, c].astype(f32)).astype(bf)
            guh[c, :] += mm_tn(gat[:, c], gh)
            gr[:, c] += mm_tn(s, gr_l)

    @pl.when(step >= tiles)
    def _():
        vd = u_h.shape[0]
        zd = aff.shape[1]
        scale = zd ** -0.5
        gsp = []
        sums = [0.0] * 4
        for b in range(RT // SPAN):
            r = slice(b * SPAN, (b + 1) * SPAN)
            p = pr[r, :]
            pf = p.astype(f32)
            ga = ascr[pl.ds(pl.multiple_of((step - tiles) * RT + b * SPAN, SPAN), SPAN), :]
            dp = mm_nt(ga, val[r, :])
            inner = jnp.sum(dp * pf, axis=-1, keepdims=True)
            gs = (pf * (dp - inner)).astype(bf)
            dq = mm(gs, qk[1, r, :]) * scale
            dk = mm_tn(gs, qk[0, r, :]) * scale
            sh = qk[2, r, :].astype(f32)
            for i, t in enumerate((dq * sh, dq, dk * sh, dk)):
                sums[i] = sums[i] + jnp.sum(t.reshape(SPAN // 8, 8, zd), axis=0)
            gsp.append(((dq * aff[0:1, :] + dk * aff[2:3, :]) * qk[3, r, :].astype(f32)).astype(bf))
            dv = mm_tn(p, ga)
            gv_o[r, :] = (dv * vsl[r, :].astype(f32)).astype(bf)
        for i in range(4):
            ga_o[i] += sums[i]
        gsp = jnp.concatenate(gsp, axis=0)
        gsp_o[...] = gsp
        gz[...] += mm_tn(sm[...], gsp)
        n = nm[...]
        for j in range(vd // 256):
            c = slice(j * 256, (j + 1) * 256)
            gv[:, c] += mm_tn(n, gv_o[:, c])

    def close():
        pack((gv, gz), give4_o, 1 - core)
        pack((gv, gz), keep4_o, core)
        three.wait("core")
        sum3_o[...] = core3[...]
        pack_add((gr,), sum3_o, core)
        two.add_y()
        sum2_o[...] = y2[...]
        piece1_o[...] = one.add_z()

    slot(2 * tiles - 1, close)


def backward_main(dm, saved, smooth, normed, affine, u_h, chunk1=None):
    rows, D = dm.shape
    vd = u_h.shape[0]
    zd = affine.shape[1]
    remote = chunk1 is not None
    tiles = rows // RT
    upd, u2, uh, val, vsl, gat, rv, a2, pr, qk = saved

    def early(width):
        return pl.BlockSpec((RT, width), lambda i: (jnp.minimum(i, tiles - 1), 0))

    def late(width):
        return pl.BlockSpec((RT, width), lambda i: (jnp.maximum(i - tiles, 0), 0))

    de, ve, vl, dl = early(D), early(vd), late(vd), late(D)
    accs = [(D, zd), (D, vd), (D, vd), (D, D), (D, D), (vd, D)]
    ga = jax.ShapeDtypeStruct((4, 8, zd), f32)
    both = pl.BlockSpec((RT, D), lambda i: (i % tiles, 0))
    ins = [(dm, de), (upd, de), (u2, de), (uh, de), (gat, ve), (rv, ve), (a2, ve), (smooth, both),
           (val, vl), (vsl, vl), (pr, late(SPAN)),
           (qk, pl.BlockSpec((4, RT, zd), lambda i: (0, jnp.maximum(i - tiles, 0), 0))), (normed, dl),
           (affine, const_spec(affine)), (u_h, const_spec(u_h))]
    wide = lambda n: jax.ShapeDtypeStruct((rows, n), bf)
    outs = [(wide(D), de), (wide(D), de), (wide(D), de), (wide(vd), ve), (wide(vd), vl), (wide(zd), late(zd)),
            (ga, const_spec(ga))]
    scratch = [pltpu.VMEM((rows, vd), bf)]
    comm = {}
    qs = ()
    if remote:
        n = [chunk1[0].shape[1], (2 * D * D + vd * D) // 4 // LG, D * vd // 4 // LG, (D * vd + D * zd) // 4 // LG]
        qs = [a // 8 for a in n]
        ins += [(c, const_spec(c)) for c in chunk1]
        buf = lambda *s: jax.ShapeDtypeStruct(s + (LG,), bf)
        outs += [(s, const_spec(s)) for s in (buf(qs[0]), buf(n[1]), buf(2, n[2]), buf(2, n[3]), buf(2, n[3]))]
        v = lambda *s: pltpu.VMEM(s + (LG,), bf)
        sem = pltpu.SemaphoreType.DMA((10,))
        scratch = [pltpu.VMEM(a, f32) for a in accs] + scratch
        scratch += [v(2, n[0]), v(n[0]), v(n[0] // 2), v(3, qs[0]), sem, sem, v(2, n[1]), v(2, n[1]), v(n[1]), sem, sem,
                    v(2, n[2]), v(2, n[2]), sem, sem]
        comm = dict(collective_id=2, has_side_effects=True)
    else:
        outs += [(s, const_spec(s)) for s in (jax.ShapeDtypeStruct(a, f32) for a in accs)]
    return pl.pallas_call(
        functools.partial(backward_kernel, qs, remote),
        grid=(2 * tiles,),
        in_specs=[i[1] for i in ins],
        out_specs=[o[1] for o in outs],
        out_shape=[o[0] for o in outs],
        scratch_shapes=scratch,
        compiler_params=pltpu.CompilerParams(vmem_limit_bytes=62 * 2**20, **comm),
        name="backward_main",
    )(*[i[0] for i in ins])


def lane_row(small, row):
    return jnp.concatenate([small[q, row:row + 1, :] for q in range(small.shape[0])], axis=1)


def input_kernel(nseq, seqlen, qs, remote, gh, gu, gr, gsp, gv, w_a, tok, small, dft, xs_i, ks_i, *rest):
    rest = list(rest)

    def take(n):
        out = rest[:n]
        del rest[:n]
        return out

    if remote:
        piece1, sum2, sum3, keep4, give4, gain1, aff = take(7)
        dn_o, full1, full2, full3, full4, small_o = take(6)
    else:
        dn_o, dema_o, dgain_o = take(3)
    dsm, dn, xr, dyspec, dxspec, gspec, dkscr = take(7)
    step = pl.program_id(0)
    ng = dsm.shape[0]
    tiles = pl.num_programs(0) - ng
    nch = seqlen // CH
    rows = nseq * seqlen
    if remote:
        f1, s1, r1 = take(3)
        x2, z2, f2, s2, r2 = take(5)
        y3, x3, z3, f3, s3, r3 = take(6)
        core4, y4, x4, z4, f4, s4, r4 = take(7)
        sums, near, total, far, s5, r5 = take(6)
        one = Reduce(qs[0], s1, r1, full=f1)
        two = Reduce(qs[1], s2, r2, y_in=sum2, x_in=x2, z_in=z2, full=f2)
        three = Reduce(qs[2], s3, r3, core_in=sum3, y_in=y3, x_in=x3, z_in=z3, full=f3)
        four = Reduce(qs[3], s4, r4, keep=keep4, give=give4, core_in=core4, y_in=y4, x_in=x4, z_in=z4, full=f4)

    def slot(at, fn):
        if remote:
            pl.when(step == at)(fn)

    def back(chunk):
        chunk.full[chunk.own_piece(), :] = chunk.add_z()
        chunk.start("back_z")

    def widen(chunk):
        chunk.wait("back_z")
        chunk.start("back_x")

    def open_up():
        greet(fsdp_peers() + dp_peers())
        f1[one.own_piece(), :] = piece1[...]
        met(10)
        three.start("y")
        one.start("back_z")
        two.start("x")
        four.start("core")

    slot(0, open_up)

    def at_two():
        four.add_core()
        four.start("y")

    slot(2, at_two)

    def at_three():
        two.add_x()
        two.start("z")
        three.add_y()
        three.start("x")
        widen(one)

    slot(3, at_three)

    @pl.when(step < tiles)
    def _():
        w_z, w_r, w_u, w_h, w_v = split_pack(w_a)
        at = pl.ds(pl.multiple_of(step * RT, RT), RT)
        x = tok[...].astype(f32)
        n = (x * lax.rsqrt(jnp.mean(x * x, axis=-1, keepdims=True) + eps)).astype(bf)
        a = mm_nt(gv[...], w_v[...])
        b = mm_nt(gh[...], w_h[...]) + mm_nt(gu[...], w_u[...]) + mm_nt(gsp[...], w_z[...]) + mm_nt(gr[...], w_r[...])
        for q in range(ng):
            c = slice(q * LG, (q + 1) * LG)
            xr[q, at, :] = n[:, c]
            dn[q, at, :] = a[:, c].astype(bf)
            dsm[q, at, :] = b[:, c].astype(bf)

    @pl.when(step >= tiles)
    def _():
        g = step - tiles

        def d_first():
            back(four)
            two.wait("back_x")

        slot(tiles + 3, d_first)
        fwd = dft[:, CH:]
        for c in range(nseq * nch):
            dyspec[c] = mm(fwd, dsm[g, c * CH:(c + 1) * CH, :])

        def a_second():
            back(two)
            three.add_x()
            three.start("z")

        slot(tiles, a_second)

        def b_first():
            four.add_y()
            four.start("x")
            one.wait("back_x")

        slot(tiles + 1, b_first)

        def c_first():
            widen(two)
            back(three)
            four.add_x()
            four.start("z")

        slot(tiles + 2, c_first)

        def d_second():
            widen(three)

        slot(tiles + 3, d_second)

        def point(i, _):
            rc = pl.ds(pl.multiple_of(i * 16, 16), 16)
            rs = pl.ds(pl.multiple_of(CH + i * 16, 16), 16)
            kc = [ks_i[d, rc, :].astype(f32) for d in range(nch)]
            ks = [ks_i[d, rs, :].astype(f32) for d in range(nch)]
            gc = [0.] * nch
            gs = [0.] * nch
            for b in range(nseq):
                dc = [dyspec[b * nch + c, rc, :] for c in range(nch)]
                ds = [dyspec[b * nch + c, rs, :] for c in range(nch)]
                for c in range(nch):
                    oc = 0.
                    os = 0.
                    for d in range(nch - c):
                        oc = oc + kc[d] * dc[c + d] + ks[d] * ds[c + d]
                        os = os + kc[d] * ds[c + d] - ks[d] * dc[c + d]
                    dxspec[b * nch + c, rc, :] = oc.astype(bf)
                    dxspec[b * nch + c, rs, :] = os.astype(bf)
                for c in range(nch):
                    xc = xs_i[b * nch + c, rc, :].astype(f32)
                    xs = xs_i[b * nch + c, rs, :].astype(f32)
                    for d in range(nch - c):
                        gc[d] = gc[d] + xc * dc[c + d] + xs * ds[c + d]
                        gs[d] = gs[d] + xc * ds[c + d] - xs * dc[c + d]
            for d in range(nch):
                gspec[d, rc, :] = gc[d].astype(bf)
                gspec[d, rs, :] = gs[d].astype(bf)
            return 0

        lax.fori_loop(0, CH // 16, point, 0)
        dgain = 0.
        for c in range(nseq * nch):
            r = slice(c * CH, (c + 1) * CH)
            t = mm_tn(fwd, dxspec[c]) + dn[g, r, :].astype(f32)
            dn_o[0, r, :] = t.astype(bf)
            dgain = dgain + jnp.sum((t * xr[g, r, :].astype(f32)).reshape(CH // 8, 8, LG), axis=0)
        for d in range(nch):
            dk = mm_tn(fwd, gspec[d])
            if d + 1 < nch:
                dk = dk + mm_tn(dft[:, :CH], gspec[d + 1])
            dkscr[d * CH:(d + 1) * CH, :] = dk * (1.0 / CH)
        p = [small[g, i * NH:(i + 1) * NH, :] for i in range(4)]
        a, gg, ex, ro, keep = ema_rates(p)
        p8 = power_of(keep, 8)
        st = [jnp.broadcast_to(p8[h:h + 1, :], (8, LG)) for h in range(NH)]

        def horner(i, ab):
            A, B = ab
            v = dkscr[pl.ds(pl.multiple_of(seqlen - 8 - i * 8, 8), 8), :]
            B = tuple(B[h] * st[h] + A[h] for h in range(NH))
            A = tuple(A[h] * st[h] + v for h in range(NH))
            return (A, B)

        none = dkscr[0:8, :] * 0.0
        zero = (none,) * NH
        A, B = lax.fori_loop(0, seqlen // 8, horner, (zero, zero), unroll=2)
        rr = lax.broadcasted_iota(jnp.int32, (8, LG), 0).astype(f32)
        As = []
        Bs = []
        for h in range(NH):
            lad = ladder(keep[h:h + 1, :], 8)
            low = jnp.concatenate([jnp.zeros((1, LG), f32), lad[:7]], axis=0)
            As.append(jnp.sum(lad * A[h], axis=0, keepdims=True))
            Bs.append(jnp.sum(rr * low * A[h] + 8.0 * lad[7:8] * lad * B[h], axis=0, keepdims=True))
        As = jnp.concatenate(As, axis=0)
        Bs = jnp.concatenate(Bs, axis=0)
        dkeep = a * ex * ro * Bs
        da = ex * ro * As - gg * dkeep
        dg = -a * dkeep
        grads = (da * a * (1.0 - a), dg * gg * (1.0 - gg), a * ro * As, a * ex * As)
        for i, v in enumerate(grads):
            if remote:
                sums[g, i * NH:(i + 1) * NH, :] = v
            else:
                dema_o[i] = v
        if remote:
            sums[g, 4 * NH:, :] = jnp.concatenate(
                [jnp.sum(dgain, axis=0, keepdims=True), jnp.zeros((7, LG), f32)], axis=0)
        else:
            dgain_o[...] = dgain

    def close():
        fs = lax.axis_index("fsdp")

        def across(k, src, dst, peer):
            return pltpu.make_async_remote_copy(src_ref=src, dst_ref=dst, send_sem=s5.at[k], recv_sem=r5.at[k],
                                                device_id=peer, device_id_type=MESH)

        g1 = jnp.sum(gain1[...], axis=0, keepdims=True)
        cols = jnp.sum(aff[...], axis=1)
        for q in range(ng):
            sums[q, 4 * NH + 1:4 * NH + 6, :] = jnp.concatenate([g1[:, q * LG:(q + 1) * LG], cols], axis=0)
        first = [across(k, sums.at[peer[1]], near.at[k], peer) for k, peer in enumerate(fsdp_peers())]
        for c in first:
            c.start()
        widen(four)
        full1[...] = f1[...]
        full2[...] = f2[...]
        for c in first:
            c.wait()
        total[...] = sums[fs] + near[0] + near[1] + near[2]
        second = [across(3 + k, total, far.at[k], peer) for k, peer in enumerate(dp_peers())]
        for c in second:
            c.start()
        three.wait("back_x")
        full3[...] = f3[...]
        for c in second:
            c.wait()
        t = total[...]
        for k in range(7):
            t = t + far[k]
        small_o[...] = t
        four.wait("back_x")
        full4[...] = f4[...]

    slot(tiles + ng - 1, close)


def input_main(grads, w_a, tokens, small, dft, xspec, kspec, nseq, comm_in=None):
    rows, D = tokens.shape
    seqlen = rows // nseq
    nch = seqlen // CH
    ng = D // LG
    nchunks = nseq * nch
    tiles = rows // RT
    remote = comm_in is not None

    def early(a):
        return pl.BlockSpec((RT, a.shape[1]), lambda i: (jnp.minimum(i, tiles - 1), 0))

    def lanes(i):
        return jnp.maximum(i - tiles, 0)

    ins = [(a, early(a)) for a in grads] + [(w_a, const_spec(w_a)), (tokens, early(tokens)), (small, const_spec(small))]
    ins += [(dft, const_spec(dft)), (xspec, pl.BlockSpec((nchunks, 2 * CH, LG), lambda i: (0, 0, lanes(i)))),
            (kspec, pl.BlockSpec((nch, 2 * CH, LG), lambda i: (0, 0, lanes(i))))]
    outs = [(jax.ShapeDtypeStruct((ng, rows, LG), bf), pl.BlockSpec((1, rows, LG), lambda i: (lanes(i), 0, 0)))]
    scratch = [pltpu.VMEM((ng, rows, LG), bf)] * 3
    scratch += [pltpu.VMEM((nchunks, 2 * CH, LG), f32),
                pltpu.VMEM((nchunks, 2 * CH, LG), bf), pltpu.VMEM((nch, 2 * CH, LG), bf), pltpu.VMEM((seqlen, LG), f32)]
    params = {}
    qs = ()
    if remote:
        piece1, sum2, sum3, keep4, give4, gain1, aff = comm_in
        n = [piece1.shape[0] * 8, sum2.shape[0], sum3.shape[1], keep4.shape[1]]
        qs = [a // 8 for a in n]
        ins += [(a, const_spec(a)) for a in comm_in]
        fulls = [jax.ShapeDtypeStruct((a, LG), bf) for a in n]
        one = jax.ShapeDtypeStruct((SMALL, LG), f32)
        outs += [(a, const_spec(a)) for a in fulls + [one]]
        v = lambda *s: pltpu.VMEM(s + (LG,), bf)
        w = lambda *s: pltpu.VMEM(s + one.shape, f32)
        sem = pltpu.SemaphoreType.DMA((10,))
        scratch += [v(n[0]), sem, sem,
                    v(n[1] // 2), v(3, qs[1]), v(n[1]), sem, sem,
                    v(n[2]), v(n[2] // 2), v(3, qs[2]), v(n[2]), sem, sem,
                    v(2, n[3]), v(n[3]), v(n[3] // 2), v(3, qs[3]), v(n[3]), sem, sem,
                    w(4), w(3), w(), w(7), sem, sem]
        params = dict(collective_id=3, has_side_effects=True)
    else:
        outs += [(jax.ShapeDtypeStruct((4, NH, D), f32), pl.BlockSpec((4, NH, LG), lambda i: (0, 0, lanes(i)))),
                 (jax.ShapeDtypeStruct((8, D), f32), pl.BlockSpec((8, LG), lambda i: (0, lanes(i))))]
    return pl.pallas_call(
        functools.partial(input_kernel, nseq, seqlen, qs, remote),
        grid=(tiles + ng,),
        in_specs=[i[1] for i in ins],
        out_specs=[o[1] for o in outs],
        out_shape=[o[0] for o in outs],
        scratch_shapes=scratch,
        compiler_params=pltpu.CompilerParams(vmem_limit_bytes=62 * 2**20, **params),
        name="input_main",
    )(*[i[0] for i in ins])


def finish_kernel(groups, fs, tok, dxd, dn, small, *rest):
    n = len(groups)
    fulls, sums = rest[:n], rest[n:n + 1]
    outs = list(rest[n + 1:] if groups else rest)
    dtok_o = outs.pop(0)
    x = tok[...].astype(f32)
    inv = lax.rsqrt(jnp.mean(x * x, axis=-1, keepdims=True) + eps)
    d = jnp.concatenate([dn[q] for q in range(dn.shape[0])], axis=1).astype(f32) * lane_row(small, 4 * NH)
    xr = x * inv
    dtok_o[...] = (dxd[...].astype(f32) + inv * (d - xr * jnp.mean(d * xr, axis=-1, keepdims=True))).astype(bf)
    if groups:
        @pl.when(pl.program_id(0) == 0)
        def _():
            gain_o, ema_o, aff_o = outs[:3]
            t = sums[0]
            gain_o[...] = t[4 * NH:4 * NH + 2, :]
            for i in range(4):
                ema_o[i] = t[i * NH:(i + 1) * NH, :]
            width = aff_o.shape[1]
            mine = 0.
            for q in range(4):
                mine = mine + jnp.where(fs[0] == q, 1.0, 0.0) * t[4 * NH + 2:4 * NH + 6, q * width:(q + 1) * width]
            aff_o[...] = mine
            at = 3
            for full, count in zip(fulls, groups):
                unpack(full, outs[at:at + count])
                at += count


def finish_main(fs, tokens, dxd, dn, small, fulls=(), sums=None, groups=(), shapes=()):
    rows, D = tokens.shape
    ng = dn.shape[0]
    ds = row_spec(D)
    extra = list(fulls) + ([sums] if groups else [])
    outs = [jax.ShapeDtypeStruct(s, f32) for s in shapes]
    return pl.pallas_call(
        functools.partial(finish_kernel, groups),
        grid=(rows // RT,),
        in_specs=[SMEM, ds, ds, pl.BlockSpec((ng, RT, LG), lambda i: (0, i, 0))] + [const_spec(a) for a in [small] + extra],
        out_specs=[ds] + [const_spec(a) for a in outs],
        out_shape=[jax.ShapeDtypeStruct((rows, D), bf)] + outs,
        name="finish",
    )(fs, tokens, dxd, dn, small, *extra)


def local_step(tokens, lengths, cotangent, fs, plain=None, shards=None):
    nseq = lengths.shape[0]
    rows, D = tokens.shape
    dft = jnp.asarray(dft_tables(), bf)
    remote = shards is not None
    if remote:
        ema_t, norm_gains, qk_affine, w_z, w_r, w_u, w_h, w_v, u_h, w_in, w_out = shards
        normed, smooth, x_spec, k_spec, small, affine, w_a, u_full = ema_forward(
            tokens, dft, nseq, comm_in=(ema_t, norm_gains, qk_affine, w_z, w_r, w_u, w_h, w_v, u_h))
        *saved, in_full, out_full = forward_main(
            lengths, smooth, normed, tokens, affine, w_a, u_full, (w_in, w_out))
    else:
        small, affine, w_a, u_full, in_full, out_full = plain
        normed, smooth, x_spec, k_spec = ema_forward(tokens, dft, nseq, small)
        saved = forward_main(lengths, smooth, normed, tokens, affine, w_a, u_full)
    middle, *saved = saved
    output, dm, g_gain1, *first = ffn_main(fs, middle, cotangent, small, in_full, out_full, remote)
    dxd, gh, gu, gr, gv, gsp, g_aff, *second = backward_main(
        dm, saved, smooth, normed, affine, u_full, first if remote else None)
    shared = ((gh, gu, gr, gsp, gv), w_a, tokens, small, dft, x_spec, k_spec, nseq)
    if not remote:
        dn, g_ema, g_gain0 = input_main(*shared)
        grad_tokens, = finish_main(fs, tokens, dxd, dn, small)
        grad_gains = jnp.stack([jnp.sum(g_gain0, axis=0), jnp.sum(g_gain1, axis=0)])
        return output, grad_tokens, (grad_gains, jnp.swapaxes(g_ema, 1, 2), jnp.sum(g_aff, axis=1), *second, *first)
    dn, *fulls, sums = input_main(*shared, (*second, g_gain1, g_aff))
    shapes = [norm_gains.shape, ema_t.shape, qk_affine.shape]
    shapes += [w.shape for w in (w_in, w_out, w_h, u_h, w_u, w_r, w_v, w_z)]
    grad_tokens, g_gains, g_ema, g_aff, g_in, g_out, g_h, g_uh, g_u, g_r, g_v, g_z = finish_main(
        fs, tokens, dxd, dn, small, fulls, sums, (2, 3, 1, 2), shapes)
    return output, grad_tokens, (g_gains, jnp.swapaxes(g_ema, 1, 2), g_aff, g_z, g_v, g_r, g_u, g_h, g_uh, g_in, g_out)


def small_table(norm_gains, ema_params):
    d = norm_gains.shape[1]
    ema = jnp.swapaxes(ema_params, 1, 2).reshape(4 * NH, d)
    rows = jnp.concatenate([ema, norm_gains, jnp.zeros((SMALL - 4 * NH - 2, d), bf)], axis=0).astype(f32)
    return jnp.swapaxes(rows.reshape(SMALL, d // LG, LG), 0, 1)


def per_device(tokens, lengths, norm_gains, ema_params, qk_affine, w_z, w_v, w_r, w_u, w_h, u_h, w_in, w_out, cotangent):
    at = lax.axis_index("fsdp")
    parts = lax.axis_size("fsdp")
    fs = at.reshape(1)
    if parts == 4 and lax.axis_size("dp") == 8:
        shards = (jnp.swapaxes(ema_params, 1, 2), norm_gains, qk_affine, w_z, w_r, w_u, w_h, w_v, u_h, w_in, w_out)
        output, grad_tokens, pieces = local_step(tokens, lengths, cotangent, fs, shards=shards)
        return (output, grad_tokens) + pieces
    gather = lambda w, axis: lax.all_gather(w, "fsdp", axis=axis, tiled=True)
    w_a = gather(jnp.concatenate([w_z, w_r, w_u, w_h, w_v], axis=1), 0)
    plain = (small_table(gather(norm_gains, 1), gather(ema_params, 1)), gather(qk_affine, 1).astype(f32), w_a,
             gather(u_h, 0), gather(w_in, 0), gather(w_out, 0))
    output, grad_tokens, totals = local_step(tokens, lengths, cotangent, fs, plain)
    summed = lax.psum(totals, ("dp", "fsdp"))
    pieces = tuple(
        lax.dynamic_slice_in_dim(g, at * (g.shape[d] // parts), g.shape[d] // parts, d)
        for g, d in zip(summed, (1, 1, 1, 0, 0, 0, 0, 0, 0, 0, 0)))
    return (output, grad_tokens) + pieces


def solution(mesh):
    rows = P(("dp", "fsdp"), None)
    shard = P("fsdp", None)
    wide = P(None, "fsdp")
    deep = P(None, "fsdp", None)
    return jax.shard_map(
        per_device,
        mesh=mesh,
        in_specs=(rows, P(("dp", "fsdp")), wide, deep, wide) + (shard,) * 8 + (rows,),
        out_specs=(rows, rows, wide, deep, wide) + (shard,) * 8,
        check_vma=False,
    )
```

time: 1270 us -> 192 us (0.15)
  matrix products: 472 us -> 0 us
  local copies, waits for them, and re-layouts: 376 us -> 0 us
  Pallas kernels: 0 us -> 191 us
  other arithmetic: 169 us -> 0 us
  waiting for transfers between devices: 144 us -> 0 us
  blocking collectives: 80.7 us -> 0 us
  between operations: 15.8 us -> 0.84 us
    dot_general x60 -> x0, matrix products: 472 us -> none  [the longest x24 170 us: advance(): jnp.einsum('sjh,bsj->bjh', absorb_table, block_in, precision=highest)]
    pallas_call x0 -> x6, Pallas kernels: none -> 191 us  [the longest x1 60 us: input_main(): pl.pallas_call(functools.partial(input_kernel, nseq, seqlen, qs, remote),...]
    psum x1 -> x0, waiting for transfers between devices: 141 us -> none  [per_device(): lax.psum((totals[0], totals[1], totals[2], totals[3], totals[4], totals[5...]
    dynamic_update_slice x8 -> x0, local copies, waits for them, and re-layouts: 116 us -> none  [smooth(): unused, states = lax.scan(jax.checkpoint(advance), initial, ordered)]
    scatter-add x1 -> x0, other arithmetic: 104 us -> none  [smooth(): jnp.take(kernel, jnp.maximum(lag_table, 0), axis=1)]
    gather x2 -> x0, local copies, waits for them, and re-layouts: 100 us -> none  [smooth(): jnp.take(kernel, jnp.maximum(lag_table, 0), axis=1)]
    psum x1 -> x0, blocking collectives: 41.6 us -> none  [per_device(): lax.psum((totals[0], totals[1], totals[2], totals[3], totals[4], totals[5...]
    all_gather x6 -> x0, blocking collectives: 39 us -> none  [the longest x1 8.16 us: per_device(): lax.all_gather(shards[7], 'fsdp', axis=0, tiled=True)]
  transfers between devices with their start and end apart: 6 -> 0, of which waited for: 1 -> 0; matrix products, arithmetic and copies ran while one was open for 32% -> 0% of each run, Pallas kernels for 0% -> 0%
where the time goes in v1:
time: 192 us
  Pallas kernels  191 us (99%)
    pallas_call x1, Pallas kernels, input_main(): pl.pallas_call(functools.partial(input_kernel, nseq, seqlen, qs, remote),...  60 us
    pallas_call x1, Pallas kernels, backward_main(): pl.pallas_call(functools.partial(backward_kernel, qs, remote), grid=(2 *...  44.4 us
    pallas_call x1, Pallas kernels, ema_forward(): pl.pallas_call(functools.partial(ema_fwd_kernel, nseq, seqlen, remote), g...  30.3 us
    pallas_call x1, Pallas kernels, forward_main(): pl.pallas_call(functools.partial(forward_kernel, rows // nseq, remote), g...  28.2 us
    pallas_call x1, Pallas kernels, ffn_main(): pl.pallas_call(functools.partial(ffn_kernel, packed), grid=(rows // RT,),...  20.7 us
    pallas_call x1, Pallas kernels, finish_main(): pl.pallas_call(functools.partial(finish_kernel, groups), grid=(rows // RT...  7.43 us

profile of v1, /device:TPU:0, one launch (start us, length us, event | category | flops | bytes accessed | tf_op | source)
XLA Modules:
  0.0 191.8 jit_solution(15493023571169534836)
XLA Ops:
  0.7 30.3 %ema_fwd.1 = (bf16[2048,512]{1,0:T(8,128)(2,1)}, bf16[2048,512]{1,0:T(8,128)(2,1)}, bf16[8,512,512]{2,1,0:T(8,128)(2,1)}, bf16[4,512,512]{2,1,0:T(8,128)(2,1)}, ...) custom-call(bf16[2048,512]{1,0:T(8,128)(2,1)} %tok.7, ...), custom_call_target="tpu_custom_call" | custom-call | tf_op jit(solution)/shard_map/ema_fwd/pallas_call | solution.py:312
  30.9 28.2 %forward_main.1 = (bf16[2048,512]{1,0:T(8,128)(2,1)}, bf16[2048,512]{1,0:T(8,128)(2,1)}, bf16[2048,512]{1,0:T(8,128)(2,1)}, bf16[2048,512]{1,0:T(8,128)(2,1)}, b...) custom-call(s32[2]{0:T(128)} %lens.1, ...), custom_call_target="tpu_custom_call" | custom-call | tf_op jit(solution)/shard_map/forward_main/pallas_call | solution.py:611
  59.1 20.7 %ffn_main.1 = (bf16[2048,512]{1,0:T(8,128)(2,1)}, bf16[2048,512]{1,0:T(8,128)(2,1)}, f32[8,512]{1,0:T(8,128)}, bf16[2,2048,128]{2,1,0:T(8,128)(2,1)}, bf16[2,2048,128]{2,1,0:T(8,128)(2,1)}) custom-call(s32[1]{0:T(128)} %bitcast.fs, bf16[2048,512]{1,0:T(8,128)(2,1)} %get-tuple-element.74.middle, bf16[2048,512]{1,0:T(8,128)(2,1)} %cot.1, ...), custom_call_target="tpu_custom_call" | custom-call | tf_op jit(solution)/shard_map/ffn_main/pallas_call | solution.py:677
  79.8 44.4 %backward_main.1 = (bf16[2048,512]{1,0:T(8,128)(2,1)}, bf16[2048,512]{1,0:T(8,128)(2,1)}, bf16[2048,512]{1,0:T(8,128)(2,1)}, bf16[2048,1024]{1,0:T(8,128)(2,1)},...) custom-call(bf16[2048,512]{1,0:T(8,128)(2,1)} %get-tuple-element.79., ...), custom_call_target="tpu_custom_call" | custom-call | tf_op jit(solution)/shard_map/backward_main/pallas_call | solution.py:871
  124.2 60.0 %input_main.1 = (bf16[4,2048,128]{2,1,0:T(8,128)(2,1)}, bf16[2048,128]{1,0:T(8,128)(2,1)}, bf16[2048,128]{1,0:T(8,128)(2,1)}, bf16[1024,128]{1,0:T(8,128)(2,1)},...) custom-call(bf16[2048,512]{1,0:T(8,128)(2,1)} %get-tuple-element.93.gh, bf16[2048,512]{1,0:T(8,128)(2,1)} %get-tuple-element.94.gu, ...), custom_call_target="tpu_custom_call" | custom-call | tf_op jit(solution)/shard_map/input_main/pallas_call | solution.py:1171
  184.2 7.4 %finish.1 = (bf16[2048,512]{1,0:T(8,128)(2,1)}, f32[2,128]{1,0:T(2,128)}, f32[4,16,128]{2,1,0:T(8,128)}, f32[4,32]{1,0:T(4,128)}, f32[128,1024]{1,0:T(8,128)}, /...) custom-call(s32[1]{0:T(128)} %bitcast.fs, ...), custom_call_target="tpu_custom_call" | custom-call | tf_op jit(solution)/shard_map/finish/pallas_call | solution.py:1218

commit v2 on v1

--- a/solution.py
+++ b/solution.py
@@ -22,7 +22,7 @@
     m=np.arange(-CH,CH)[None,:]
     ang=2*np.pi*f*m/(2*CH)
     both=np.concatenate([np.cos(ang),np.sin(ang)],axis=0)
-    return both.astype(np.float32)
+    return np.concatenate([both,both.T],axis=0).astype(np.float32)
 
 def mm(a,b): return jnp.dot(a,b,preferred_element_type=f32)
 def mm_tn(a,b): return lax.dot_general(a,b,(((0,),(0,)),((),())),preferred_element_type=f32)
@@ -74,35 +74,46 @@
         self.dp = lax.axis_index("dp")
         self.fs = lax.axis_index("fsdp")
         self.x = self.dp % 2
+        self.z = (self.dp // 2) % 2
         self.core_peer = (self.dp, flip(self.fs, 1))
         self.y_peer = (self.dp, flip(self.fs, 2))
         self.x_peer = (flip(self.dp, 1), self.fs)
+        self.z_peer = (flip(self.dp, 2), self.fs)
 
     def peers(self):
-        return [self.core_peer, self.y_peer, self.x_peer]
+        return [self.core_peer, self.y_peer, self.x_peer, self.z_peer]
 
     def copy(self, p, k):
-        a, first, r = self.pieces[p]
+        a, col, width = self.pieces[p]
         shard, out = self.shards[a], self.outs[a]
         n = shard.shape[0]
-        h = n // 2
-        half = self.x * h + first
-        other = (1 - self.x) * h + first
         far = flip(self.fs, 2) * n
-        at = lambda ref, row: ref.at[pl.ds(pl.multiple_of(row, r), r)]
+        cols = pl.ds(col, width)
+        x, z = self.x, self.z
+
+        def at(ref, base, zz, xx, half=None):
+            r = n // 4 if half is None else n // 8
+            row = base + (2 * zz + xx) * (n // 4) + (0 if half is None else half * r)
+            return ref.at[pl.ds(pl.multiple_of(row, r), r), cols]
+
         src, dst, peer = (
-            (at(shard, half), at(out, self.fs * n + half), self.y_peer),
-            (at(out, far + half), at(out, far + half), self.x_peer),
-            (at(out, far + half), at(out, far + half), self.core_peer),
-            (at(out, far + other), at(out, far + other), self.core_peer),
+            (at(shard, 0, z, x), at(out, self.fs * n, z, x), self.y_peer),
+            (at(out, far, z, x),) * 2 + (self.x_peer,),
+            (at(out, far, z, x),) * 2 + (self.z_peer,),
+            (at(out, far, 1 - z, x, 0),) * 2 + (self.x_peer,),
+            (at(out, far, z, 1 - x, 1),) * 2 + (self.z_peer,),
+            (at(out, far, z, x),) * 2 + (self.core_peer,),
+            (at(out, far, z, 1 - x),) * 2 + (self.core_peer,),
+            (at(out, far, 1 - z, x),) * 2 + (self.core_peer,),
+            (at(out, far, 1 - z, 1 - x),) * 2 + (self.core_peer,),
         )[k]
         return pltpu.make_async_remote_copy(
-            src_ref=src, dst_ref=dst, send_sem=self.send.at[4 * p + k], recv_sem=self.recv.at[4 * p + k],
+            src_ref=src, dst_ref=dst, send_sem=self.send.at[9 * p + k], recv_sem=self.recv.at[9 * p + k],
             device_id=peer, device_id_type=MESH)
 
     def whole(self, a):
         n = self.shards[a].shape[0]
-        slot = 4 * len(self.pieces) + a
+        slot = 9 * len(self.pieces) + a
         return pltpu.make_async_remote_copy(
             src_ref=self.shards[a], dst_ref=self.outs[a].at[pl.ds(pl.multiple_of(self.fs * n, n), n)],
             send_sem=self.send.at[slot], recv_sem=self.recv.at[slot], device_id=self.core_peer, device_id_type=MESH)
@@ -121,18 +132,27 @@
 
     def relay(self, p):
         self.copy(p, 0).wait_recv()
-        self.copy(p, 1).start()
-        self.copy(p, 2).start()
+        for k in (1, 2, 5):
+            self.copy(p, k).start()
+
+    def cross(self, p):
+        self.copy(p, 2).wait_recv()
+        self.copy(p, 3).start()
+        self.copy(p, 7).start()
+        self.copy(p, 1).wait_recv()
+        self.copy(p, 4).start()
+        self.copy(p, 6).start()
 
     def last(self, p):
-        self.copy(p, 1).wait_recv()
-        self.copy(p, 3).start()
+        self.copy(p, 3).wait_recv()
+        self.copy(p, 4).wait_recv()
+        self.copy(p, 8).start()
 
     def finish(self):
         for p in range(len(self.pieces)):
-            for k in range(4):
+            for k in range(9):
                 self.copy(p, k).wait_send()
-            for k in (2, 3):
+            for k in (5, 6, 7, 8):
                 self.copy(p, k).wait_recv()
         for a in range(len(self.shards)):
             self.whole(a).wait()
@@ -140,12 +160,12 @@
 
 
 def gather_sems(arrays, pieces):
-    sem = pltpu.SemaphoreType.DMA((4 * pieces + arrays,))
+    sem = pltpu.SemaphoreType.DMA((9 * pieces + arrays,))
     return [sem, sem, pltpu.SemaphoreType.DMA((arrays,))]
 
 
-SMALL = 4 * NH + 8
-PIECES = ((0, 0, 32), (0, 32, 32), (1, 0, 128))
+SMALL = 4 * NH + 16
+PIECES = 3
 
 
 def ema_fwd_kernel(nseq, seqlen, remote, tok, dft, *rest):
@@ -168,11 +188,12 @@
         small_o, aff_o, w_full, u_full = take(4)
     nscr, kscr, kspec, xspec, yspec = take(5)
     if remote:
-        small, own, s1, r1, *sems = take(7)
+        small, sent, own, s1, r1, *sems = take(8)
         fs = lax.axis_index("fsdp")
-        gather = Gather((own, parts[5]), (w_full, u_full), PIECES, *sems)
+        gather = Gather((own, parts[5]), (w_full, u_full),
+                        ((0, 0, 1664), (0, 1664, own.shape[1] - 1664), (1, 0, parts[5].shape[1])), *sems)
         across = [pltpu.make_async_remote_copy(
-            src_ref=small.at[fs], dst_ref=small.at[fs], send_sem=s1.at[k], recv_sem=r1.at[k],
+            src_ref=sent.at[fs], dst_ref=sent.at[fs], send_sem=s1.at[k], recv_sem=r1.at[k],
             device_id=peer, device_id_type=MESH) for k, peer in enumerate(fsdp_peers())]
 
     def slot(at, fn):
@@ -180,17 +201,17 @@
             pl.when(g == at)(fn)
 
     def open_up():
-        greet(fsdp_peers() + [gather.x_peer])
+        greet(fsdp_peers() + [gather.x_peer, gather.z_peer])
         for i in range(4):
-            small[fs, i * NH:(i + 1) * NH, :] = ema_i[i].astype(f32)
+            sent[fs, i * NH:(i + 1) * NH, :] = ema_i[i]
         tail = [gain_i[...].astype(f32), jnp.concatenate([aff_i[...].astype(f32)] * 4, axis=1),
-                jnp.zeros((2, LG), f32)]
-        small[fs, 4 * NH:, :] = jnp.concatenate(tail, axis=0)
+                jnp.zeros((SMALL - 4 * NH - 6, LG), f32)]
+        sent[fs, 4 * NH:, :] = jnp.concatenate(tail, axis=0).astype(bf)
         at = 0
         for w in parts[:5]:
             own[:, at:at + w.shape[1]] = w[...]
             at += w.shape[1]
-        met(4)
+        met(5)
         for c in across:
             c.start()
         gather.begin()
@@ -211,15 +232,23 @@
     def settle():
         for c in across:
             c.wait()
+        for q in range(4):
+            small[q] = sent[q].astype(f32)
         small_o[...] = small[...]
         for q in range(4):
             n = aff_i.shape[1]
             aff_o[:, q * n:(q + 1) * n] = small[q, 4 * NH + 2:4 * NH + 6, 0:n]
 
     slot(0, settle)
-    slot(1, lambda: gather.relay(0))
-    slot(2, lambda: gather.relay(1))
-    slot(3, lambda: gather.relay(2))
+
+    slot(1, lambda: gather.relay(1))
+    slot(2, lambda: gather.cross(1))
+
+    def last_first():
+        gather.last(0)
+        gather.last(1)
+
+    slot(3, last_first)
     p = [small[g, i * NH:(i + 1) * NH, :] for i in range(4)]
     normed = (nscr[g] * small[g, 4 * NH:4 * NH + 1, :]).astype(bf)
     normed_o[...] = normed
@@ -233,26 +262,31 @@
         st.append(jnp.broadcast_to(step[h:h + 1, :], (8, LG)))
 
     def kgen(i, zs):
-        acc = zs[0]
-        for h in range(1, NH):
-            acc = acc + zs[h]
+        acc = list(zs)
+        while len(acc) > 1:
+            acc = [acc[j] + acc[j + 1] for j in range(0, len(acc), 2)]
+        acc = acc[0]
         kscr[pl.ds(pl.multiple_of(CH + i * 16, 16), 16), :] = acc.astype(bf)
         return tuple(jnp.concatenate([zs[h][:8] * st[h], zs[h][8:] * st[h]], axis=0) for h in range(NH))
 
-    lax.fori_loop(0, seqlen // 16, kgen, tuple(z0), unroll=2)
+    lax.fori_loop(0, seqlen // 16, kgen, tuple(z0), unroll=4)
     kscr[0:CH, :] = jnp.zeros((CH, LG), bf)
-    for d in range(nch):
-        kd = mm(dft[...], kscr[d * CH:(d + 2) * CH, :])
-        kspec[d] = kd
-        ks_o[d] = kd.astype(bf)
-    fwd = dft[:, CH:]
-    for c in range(nseq * nch):
-        xd = mm(fwd, normed[c * CH:(c + 1) * CH, :])
-        xspec[c] = xd
-        xs_o[c] = xd.astype(bf)
-
-    slot(2, lambda: gather.last(0))
-    slot(3, lambda: gather.last(1))
+    both = dft[:2 * CH]
+    fwd = dft[:2 * CH, CH:]
+    inv = dft[3 * CH:]
+    for d in range(0, nch, 2):
+        kd = mm(both, jnp.concatenate([kscr[d * CH:(d + 2) * CH, :], kscr[(d + 1) * CH:(d + 3) * CH, :]], axis=1))
+        for i in range(2):
+            kspec[d + i] = kd[:, i * LG:(i + 1) * LG]
+            ks_o[d + i] = kd[:, i * LG:(i + 1) * LG].astype(bf)
+    for c in range(0, nseq * nch, 2):
+        xd = mm(fwd, jnp.concatenate([normed[c * CH:(c + 1) * CH], normed[(c + 1) * CH:(c + 2) * CH]], axis=1))
+        for i in range(2):
+            xspec[c + i] = xd[:, i * LG:(i + 1) * LG]
+            xs_o[c + i] = xd[:, i * LG:(i + 1) * LG].astype(bf)
+
+    slot(1, lambda: gather.relay(2))
+    slot(2, lambda: gather.cross(2))
 
     def point(i, _):
         rc = pl.ds(pl.multiple_of(i * 16, 16), 16)
@@ -273,8 +307,12 @@
         return 0
 
     lax.fori_loop(0, CH // 16, point, 0)
-    for c in range(nseq * nch):
-        smooth_o[c * CH:(c + 1) * CH, :] = mm_tn(fwd, yspec[c]).astype(bf)
+    slot(0, lambda: gather.relay(0))
+    slot(1, lambda: gather.cross(0))
+    for c in range(0, nseq * nch, 2):
+        y = mm(inv, jnp.concatenate([yspec[c], yspec[c + 1]], axis=1)).astype(bf)
+        smooth_o[c * CH:(c + 1) * CH, :] = y[:, :LG]
+        smooth_o[(c + 1) * CH:(c + 2) * CH, :] = y[:, LG:]
 
     def close():
         gather.last(2)
@@ -307,7 +345,7 @@
         outs += [(a, const_spec(a)), (b, const_spec(b)), (jax.ShapeDtypeStruct((D, n), bf), ANY),
                  (jax.ShapeDtypeStruct((4 * u.shape[0], D), bf), ANY)]
         sem = pltpu.SemaphoreType.DMA((3,))
-        scratch += [pltpu.VMEM(a.shape, f32), pltpu.VMEM((D // 4, n), bf), sem, sem] + gather_sems(2, len(PIECES))
+        scratch += [pltpu.VMEM(a.shape, f32), pltpu.VMEM(a.shape, bf), pltpu.VMEM((D // 4, n), bf), sem, sem] + gather_sems(2, PIECES)
         params = dict(collective_id=1, has_side_effects=True)
     return pl.pallas_call(
         functools.partial(ema_fwd_kernel, nseq, seqlen, remote),
@@ -322,8 +360,8 @@
 
 
 class Reduce:
-    def __init__(self, q, send, recv, **refs):
-        self.q, self.send, self.recv = q, send, recv
+    def __init__(self, q, first, send, recv, **refs):
+        self.q, self.first, self.send, self.recv = q, first, send, recv
         self.__dict__.update(refs)
         self.dp = lax.axis_index("dp")
         self.fs = lax.axis_index("fsdp")
@@ -333,6 +371,9 @@
 
     def rows(self, at, count):
         return pl.ds(pl.multiple_of(at, self.q), count)
+
+    def half(self, x):
+        return self.rows(x * 4 * self.q, 4 * self.q)
 
     def remote(self, src, dst, slot, device):
         return pltpu.make_async_remote_copy(
@@ -350,21 +391,27 @@
 
     def copies(self, stage):
         q = self.q
+        over_y = (self.dp, flip(self.fs, 2))
+        over_x = (flip(self.dp, 1), self.fs)
         if stage == "core":
             return [self.remote(self.give, self.core_in, 0, (self.dp, flip(self.fs, 1)))]
-        if stage == "y":
-            return [self.remote(self.core_in.at[1 - self.y], self.y_in, 1, (self.dp, flip(self.fs, 2)))]
-        if stage == "x":
-            return [self.remote(self.y_in.at[self.rows((1 - self.x) * 4 * q, 4 * q)], self.x_in, 2,
-                                (flip(self.dp, 1), self.fs))]
+        if stage == "near" and self.first == "y":
+            return [self.remote(self.core_in.at[1 - self.y], self.near, 1, over_y)]
+        if stage == "near":
+            return [self.remote(self.core_in.at[y, self.half(1 - self.x)], self.near.at[y], 1 + y, over_x)
+                    for y in range(2)]
+        if stage == "next" and self.first == "y":
+            return [self.remote(self.near.at[self.half(1 - self.x)], self.mid, 3, over_x)]
+        if stage == "next":
+            return [self.remote(self.near.at[1 - self.y], self.mid, 3, over_y)]
         if stage == "z":
-            return [self.remote(self.x_in.at[self.rows((dp // 2) * q, q)], self.z_in.at[i], 3 + i, (dp, self.fs))
+            return [self.remote(self.mid.at[self.rows((dp // 2) * q, q)], self.z_in.at[i], 4 + i, (dp, self.fs))
                     for i, dp in self.line()]
         if stage == "back_z":
             mine = self.full.at[self.own_piece()]
-            return [self.remote(mine, mine, 6 + i, (dp, self.fs)) for i, dp in self.line()]
-        half = self.full.at[self.rows(self.x * 4 * q, 4 * q)]
-        return [self.remote(half, half, 9, (flip(self.dp, 1), self.fs))]
+            return [self.remote(mine, mine, 7 + i, (dp, self.fs)) for i, dp in self.line()]
+        half = self.full.at[self.half(self.x)]
+        return [self.remote(half, half, 10, over_x)]
 
     def start(self, stage):
         for c in self.copies(stage):
@@ -374,41 +421,50 @@
         for c in self.copies(stage):
             c.wait()
 
-    def add_core(self):
-        self.wait("core")
-        step = 2 * self.q
-        for y in range(2):
-            @pl.loop(0, 4)
-            def _(i):
-                r = pl.ds(pl.multiple_of(i * step, step), step)
-                self.core_in[y, r, :] = (self.core_in[y, r, :].astype(f32) + self.keep[y, r, :].astype(f32)).astype(bf)
-
-    def add_y(self):
-        self.wait("y")
-        step = 2 * self.q
-
+    def add(self, dst, src, count):
         @pl.loop(0, 4)
         def _(i):
-            r = pl.ds(pl.multiple_of(i * step, step), step)
-            self.y_in[r, :] = (self.y_in[r, :].astype(f32) + self.core_in[self.y, r, :].astype(f32)).astype(bf)
-
-    def add_x(self):
-        self.wait("x")
-        q = self.q
-
-        @pl.loop(0, 4)
-        def _(i):
-            r = self.rows(i * q, q)
-            k = self.rows((self.x * 4 + i) * q, q)
-            self.x_in[r, :] = (self.x_in[r, :].astype(f32) + self.y_in[k, :].astype(f32)).astype(bf)
+            r = self.rows(i * (count // 4), count // 4)
+            dst[r, :] = (dst[r, :].astype(f32) + src[r, :].astype(f32)).astype(bf)
+
+    def to_near(self):
+        self.wait("core")
+        for y in range(2):
+            self.add(self.core_in.at[y], self.keep.at[y], 8 * self.q)
+        self.start("near")
+
+    def add_near(self):
+        self.wait("near")
+        if self.first == "y":
+            self.add(self.near, self.core_in.at[self.y], 8 * self.q)
+        else:
+            for y in range(2):
+                self.add(self.near.at[y], self.core_in.at[y, self.half(self.x)], 4 * self.q)
+
+    def to_next(self):
+        self.add_near()
+        self.start("next")
+
+    def to_z(self):
+        self.wait("next")
+        src = self.near.at[self.half(self.x)] if self.first == "y" else self.near.at[self.y]
+        self.add(self.mid, src, 4 * self.q)
+        self.start("z")
 
     def add_z(self):
         self.wait("z")
-        q = self.q
-        total = self.x_in[self.rows(self.z * q, q), :].astype(f32)
+        total = self.mid[self.rows(self.z * self.q, self.q), :].astype(f32)
         for i in range(3):
             total += self.z_in[i].astype(f32)
         return total.astype(bf)
+
+    def back(self):
+        self.full[self.own_piece(), :] = self.add_z()
+        self.start("back_z")
+
+    def widen(self):
+        self.wait("back_z")
+        self.start("back_x")
 
     def own_piece(self):
         return self.rows((self.x * 4 + self.z) * self.q, self.q)
@@ -473,6 +529,7 @@
 
 
 RT = 512
+TT = 1024
 
 
 def sigm(v):
@@ -498,7 +555,7 @@
     middle_o, upd_o, u2_o, uh_o, val_o, vsl_o, gat_o, rv_o, a2_o, pr_o, qk_o = rest[:11]
     rest = rest[11:]
     if remote:
-        gather = Gather(shards, rest[:2], ((0, 0, 64), (1, 0, 128)), *rest[3:])
+        gather = Gather(shards, rest[:2], tuple((a, 0, w.shape[1]) for a, w in enumerate(shards)), *rest[3:])
         rest = rest[2:]
     gscr = rest[0]
 
@@ -535,6 +592,30 @@
         p = (e / jnp.sum(e, axis=-1, keepdims=True)).astype(bf)
         pr_o[r, :] = p
         probs.append(p)
+
+    def begin():
+        met(4)
+        gather.begin()
+
+    slot(0, begin)
+
+    def relay():
+        gather.relay(0)
+        gather.relay(1)
+
+    slot(1, relay)
+
+    def cross():
+        gather.cross(0)
+        gather.cross(1)
+
+    slot(2, cross)
+
+    def last():
+        gather.last(0)
+        gather.last(1)
+
+    slot(3, last)
     rows = base + lax.broadcasted_iota(jnp.int32, (RT, 1), 0)
     live = (rows < length).astype(f32)
     for j in range(vd // 256):
@@ -571,21 +652,6 @@
         uh_o[:, c] = (up * (sg + cand - cand * sg)).astype(bf)
 
 
-    def begin():
-        met(3)
-        gather.begin()
-
-    def relay():
-        gather.relay(0)
-        gather.relay(1)
-
-    def last():
-        gather.last(0)
-        gather.last(1)
-
-    slot(0, begin)
-    slot(1, relay)
-    slot(2, last)
     slot(3, lambda: gather.finish())
 
 
@@ -624,7 +690,7 @@
 
 def ffn_kernel(packed, fs, middle, cot, gain, w_in, w_out, out_o, dm_o, dg_o, *rest):
     if packed:
-        keep_o, give_o, gwi, gwo, ascr, gscr = rest
+        keep_a, give_a, keep_b, give_b, gwi, gwo, ascr, gscr = rest
     else:
         gwi, gwo, ascr, gscr = rest
 
@@ -654,7 +720,7 @@
         gwi[:, c] += mm_tn(y, gf)
     out_o[...] = (m + mm(ascr[...], w_out[...])).astype(bf)
     dy = mm_nt(gscr[...], w_in[...])
-    dg_o[...] += jnp.sum((dy * mr).reshape(RT // 8, 8, m.shape[1]), axis=0)
+    dg_o[...] += jnp.sum((dy * mr).reshape(TT // 8, 8, m.shape[1]), axis=0)
     dyg = dy * gn
     inner = jnp.mean(dyg * mr, axis=-1, keepdims=True)
     dm_o[...] = (cl.astype(f32) + inv * (dyg - mr * inner)).astype(bf)
@@ -662,26 +728,28 @@
         @pl.when(pl.program_id(0) == pl.num_programs(0) - 1)
         def _():
             core = fs[0] % 2
-            pack((gwi, gwo), give_o, 1 - core)
-            pack((gwi, gwo), keep_o, core)
+            pack((gwo,), give_a, 1 - core)
+            pack((gwo,), keep_a, core)
+            pack((gwi,), give_b, 1 - core)
+            pack((gwi,), keep_b, core)
 
 
 def ffn_main(fs, middle, cot, gains, w_in, w_out, packed):
     rows, D = middle.shape
     ff = w_in.shape[1]
-    ds = row_spec(D)
+    ds = pl.BlockSpec((TT, D), lambda i: (i, 0))
     accs = [(D, ff), (ff, D)]
-    pair = [jax.ShapeDtypeStruct((2, (D * ff + ff * D) // 4 // LG, LG), bf)] * 2
+    pair = [jax.ShapeDtypeStruct((2, D * ff // 4 // LG, LG), bf)] * 4
     extra = pair if packed else [jax.ShapeDtypeStruct(s, f32) for s in accs]
     gain = jax.ShapeDtypeStruct((8, D), f32)
     return pl.pallas_call(
         functools.partial(ffn_kernel, packed),
-        grid=(rows // RT,),
+        grid=(rows // TT,),
         in_specs=[SMEM, ds, ds] + [const_spec(w) for w in (gains, w_in, w_out)],
         out_specs=[ds, ds] + [const_spec(a) for a in [gain] + extra],
         out_shape=[jax.ShapeDtypeStruct((rows, D), bf)] * 2 + [gain] + extra,
         scratch_shapes=([pltpu.VMEM(s, f32) for s in accs] if packed else [])
-        + [pltpu.VMEM((RT, ff), bf), pltpu.VMEM((RT, ff), bf)],
+        + [pltpu.VMEM((TT, ff), bf), pltpu.VMEM((TT, ff), bf)],
         compiler_params=pltpu.CompilerParams(vmem_limit_bytes=60 * 2**20),
         name="ffn_main",
     )(fs, middle, cot, gains, w_in, w_out)
@@ -696,22 +764,25 @@
         return out
 
     if remote:
-        keep1, give1 = take(2)
+        keep_a, give_a, keep_b, give_b = take(4)
     dxd_o, gh_o, gu_o, gr_o, gv_o, gsp_o, ga_o = take(7)
     if remote:
-        piece1_o, sum2_o, sum3_o, keep4_o, give4_o = take(5)
+        half_a_o, piece_b_o, near_c_o, near_d_o, keep_e_o, give_e_o = take(6)
     gz, gv, gr, gu, gh_w, guh = take(6)
     ascr, = take(1)
     step = pl.program_id(0)
     tiles = pl.num_programs(0) // 2
     if remote:
-        core1, y1, x1, z1, s1, r1 = take(6)
-        give2, core2, y2, s2, r2 = take(5)
-        give3, core3, s3, r3 = take(4)
-        one = Reduce(qs[0], s1, r1, keep=keep1, give=give1, core_in=core1, y_in=y1, x_in=x1, z_in=z1)
-        two = Reduce(qs[1], s2, r2, give=give2, core_in=core2, y_in=y2)
-        three = Reduce(qs[2], s3, r3, give=give3, core_in=core3)
-        core = lax.axis_index("fsdp") % 2
+        core1, near1, mid1, z1, f1, s1, r1 = take(7)
+        core2, near2, mid2, z2, s2, r2 = take(6)
+        give3, core3, near3, s3, r3 = take(5)
+        give4, core4, near4, s4, r4 = take(5)
+        a = Reduce(qs[0], "y", s1, r1, keep=keep_a, give=give_a, core_in=core1, near=near1, mid=mid1, z_in=z1, full=f1)
+        b = Reduce(qs[1], "x", s2, r2, keep=keep_b, give=give_b, core_in=core2, near=near2, mid=mid2, z_in=z2)
+        c = Reduce(qs[2], "y", s3, r3, give=give3, core_in=core3, near=near3)
+        d = Reduce(qs[3], "x", s4, r4, give=give4, core_in=core4, near=near4)
+        core = a.fs % 2
+        ra, rb, rd = a, b, d
 
     def slot(at, fn):
         if remote:
@@ -723,40 +794,35 @@
             o[...] = jnp.zeros_like(o)
 
     def open_up():
-        greet(fsdp_peers() + dp_peers())
-        met(10)
-        one.start("core")
+        greet(fsdp_peers()[:2] + dp_peers())
+        met(9)
+        a.start("core")
+        b.start("core")
 
     slot(0, open_up)
 
-    def first():
-        one.add_core()
-        one.start("y")
-
-    slot(1, first)
-
-    def second():
-        pack((gh_w, guh, gu), give2, 1 - core)
-        two.start("core")
-        one.add_y()
-        one.start("x")
-
-    slot(tiles, second)
-
-    def third():
-        two.wait("core")
-        pack_add((gh_w, guh, gu), core2, core)
-        two.start("y")
-        pack((gr,), give3, 1 - core)
-        three.start("core")
-
-    slot(tiles + 1, third)
-
-    def fourth():
-        one.add_x()
-        one.start("z")
-
-    slot(tiles + 3, fourth)
+    def at_one():
+        a.to_near()
+        b.to_near()
+
+    slot(1, at_one)
+
+    def send_core(chunk, accs):
+        pack(accs, chunk.give, 1 - core)
+        chunk.start("core")
+
+    def send_near(chunk, accs):
+        chunk.wait("core")
+        pack_add(accs, chunk.core_in, core)
+        chunk.start("near")
+
+    def at_four():
+        send_core(c, (gr, gh_w))
+        send_core(d, (guh, gu))
+
+    slot(tiles, at_four)
+    slot(tiles + 1, lambda: send_near(c, (gr, gh_w)))
+    slot(tiles + 3, lambda: a.back())
 
     @pl.when(step < tiles)
     def _():
@@ -770,6 +836,12 @@
         s = sm[...]
         gh_w[...] += mm_tn(s, gh)
         gu[...] += mm_tn(s, gu_l)
+
+        def onward():
+            ra.to_next()
+            rb.to_next()
+
+        slot(3, onward)
         at = pl.ds(pl.multiple_of(step * RT, RT), RT)
         for j in range(vd // 256):
             c = slice(j * 256, (j + 1) * 256)
@@ -806,6 +878,13 @@
         for i in range(4):
             ga_o[i] += sums[i]
         gsp = jnp.concatenate(gsp, axis=0)
+
+        def middle():
+            ra.to_z()
+            rb.to_z()
+
+        slot(tiles, middle)
+        slot(tiles + 1, lambda: send_near(rd, (guh, gu)))
         gsp_o[...] = gsp
         gz[...] += mm_tn(sm[...], gsp)
         n = nm[...]
@@ -814,23 +893,24 @@
             gv[:, c] += mm_tn(n, gv_o[:, c])
 
     def close():
-        pack((gv, gz), give4_o, 1 - core)
-        pack((gv, gz), keep4_o, core)
-        three.wait("core")
-        sum3_o[...] = core3[...]
-        pack_add((gr,), sum3_o, core)
-        two.add_y()
-        sum2_o[...] = y2[...]
-        piece1_o[...] = one.add_z()
+        pack((gv, gz), give_e_o, 1 - core)
+        pack((gv, gz), keep_e_o, core)
+        c.add_near()
+        near_c_o[...] = near3[...]
+        d.add_near()
+        near_d_o[...] = near4[...]
+        a.wait("back_z")
+        half_a_o[...] = f1[a.half(a.x), :]
+        piece_b_o[...] = b.add_z()
 
     slot(2 * tiles - 1, close)
 
 
-def backward_main(dm, saved, smooth, normed, affine, u_h, chunk1=None):
+def backward_main(dm, saved, smooth, normed, affine, u_h, chunks=None):
     rows, D = dm.shape
     vd = u_h.shape[0]
     zd = affine.shape[1]
-    remote = chunk1 is not None
+    remote = chunks is not None
     tiles = rows // RT
     upd, u2, uh, val, vsl, gat, rv, a2, pr, qk = saved
 
@@ -855,16 +935,20 @@
     comm = {}
     qs = ()
     if remote:
-        n = [chunk1[0].shape[1], (2 * D * D + vd * D) // 4 // LG, D * vd // 4 // LG, (D * vd + D * zd) // 4 // LG]
+        n = [chunks[0].shape[1], chunks[2].shape[1], (D * vd + D * D) // 4 // LG, (vd * D + D * D) // 4 // LG,
+             (D * vd + D * zd) // 4 // LG]
         qs = [a // 8 for a in n]
-        ins += [(c, const_spec(c)) for c in chunk1]
+        ins += [(c, const_spec(c)) for c in chunks]
         buf = lambda *s: jax.ShapeDtypeStruct(s + (LG,), bf)
-        outs += [(s, const_spec(s)) for s in (buf(qs[0]), buf(n[1]), buf(2, n[2]), buf(2, n[3]), buf(2, n[3]))]
+        outs += [(s, const_spec(s)) for s in (buf(n[0] // 2), buf(qs[1]), buf(n[2]), buf(2, n[3] // 2), buf(2, n[4]),
+                                              buf(2, n[4]))]
         v = lambda *s: pltpu.VMEM(s + (LG,), bf)
-        sem = pltpu.SemaphoreType.DMA((10,))
+        sem = pltpu.SemaphoreType.DMA((11,))
         scratch = [pltpu.VMEM(a, f32) for a in accs] + scratch
-        scratch += [v(2, n[0]), v(n[0]), v(n[0] // 2), v(3, qs[0]), sem, sem, v(2, n[1]), v(2, n[1]), v(n[1]), sem, sem,
-                    v(2, n[2]), v(2, n[2]), sem, sem]
+        scratch += [v(2, n[0]), v(n[0]), v(n[0] // 2), v(3, qs[0]), v(n[0]), sem, sem,
+                    v(2, n[1]), v(2, n[1] // 2), v(n[1] // 2), v(3, qs[1]), sem, sem,
+                    v(2, n[2]), v(2, n[2]), v(n[2]), sem, sem,
+                    v(2, n[3]), v(2, n[3]), v(2, n[3] // 2), sem, sem]
         comm = dict(collective_id=2, has_side_effects=True)
     else:
         outs += [(s, const_spec(s)) for s in (jax.ShapeDtypeStruct(a, f32) for a in accs)]
@@ -893,8 +977,8 @@
         return out
 
     if remote:
-        piece1, sum2, sum3, keep4, give4, gain1, aff = take(7)
-        dn_o, full1, full2, full3, full4, small_o = take(6)
+        half_a, piece_b, near_c, near_d, keep_e, give_e, gain1, aff = take(8)
+        dn_o, full_a, full_b, full_c, full_d, full_e, small_o = take(7)
     else:
         dn_o, dema_o, dgain_o = take(3)
     dsm, dn, xr, dyspec, dxspec, gspec, dkscr = take(7)
@@ -904,51 +988,47 @@
     nch = seqlen // CH
     rows = nseq * seqlen
     if remote:
+        f0, s0, r0 = take(3)
         f1, s1, r1 = take(3)
-        x2, z2, f2, s2, r2 = take(5)
-        y3, x3, z3, f3, s3, r3 = take(6)
-        core4, y4, x4, z4, f4, s4, r4 = take(7)
-        sums, near, total, far, s5, r5 = take(6)
-        one = Reduce(qs[0], s1, r1, full=f1)
-        two = Reduce(qs[1], s2, r2, y_in=sum2, x_in=x2, z_in=z2, full=f2)
-        three = Reduce(qs[2], s3, r3, core_in=sum3, y_in=y3, x_in=x3, z_in=z3, full=f3)
-        four = Reduce(qs[3], s4, r4, keep=keep4, give=give4, core_in=core4, y_in=y4, x_in=x4, z_in=z4, full=f4)
+        mid2, z2, f2, s2, r2 = take(5)
+        mid3, z3, f3, s3, r3 = take(5)
+        core4, near4, mid4, z4, f4, s4, r4 = take(7)
+        sums, near, total, far, s5, r5, gains = take(7)
+        a_ = Reduce(qs[0], "y", s0, r0, full=f0)
+        b_ = Reduce(qs[1], "x", s1, r1, full=f1)
+        c_ = Reduce(qs[2], "y", s2, r2, near=near_c, mid=mid2, z_in=z2, full=f2)
+        d_ = Reduce(qs[3], "x", s3, r3, near=near_d, mid=mid3, z_in=z3, full=f3)
+        e_ = Reduce(qs[4], "y", s4, r4, keep=keep_e, give=give_e, core_in=core4, near=near4, mid=mid4, z_in=z4, full=f4)
 
     def slot(at, fn):
         if remote:
             pl.when(step == at)(fn)
 
-    def back(chunk):
-        chunk.full[chunk.own_piece(), :] = chunk.add_z()
-        chunk.start("back_z")
-
-    def widen(chunk):
-        chunk.wait("back_z")
-        chunk.start("back_x")
-
     def open_up():
         greet(fsdp_peers() + dp_peers())
-        f1[one.own_piece(), :] = piece1[...]
+        f0[a_.half(a_.x), :] = half_a[...]
+        f1[b_.own_piece(), :] = piece_b[...]
         met(10)
-        three.start("y")
-        one.start("back_z")
-        two.start("x")
-        four.start("core")
+        c_.start("next")
+        d_.start("next")
+        e_.start("core")
+        b_.start("back_z")
 
     slot(0, open_up)
 
+    def at_one():
+        e_.to_near()
+        a_.start("back_x")
+
+    slot(1, at_one)
+
     def at_two():
-        four.add_core()
-        four.start("y")
+        c_.to_z()
 
     slot(2, at_two)
-
     def at_three():
-        two.add_x()
-        two.start("z")
-        three.add_y()
-        three.start("x")
-        widen(one)
+        d_.to_z()
+        b_.widen()
 
     slot(3, at_three)
 
@@ -970,41 +1050,28 @@
     def _():
         g = step - tiles
 
-        def d_first():
-            back(four)
-            two.wait("back_x")
-
-        slot(tiles + 3, d_first)
-        fwd = dft[:, CH:]
-        for c in range(nseq * nch):
-            dyspec[c] = mm(fwd, dsm[g, c * CH:(c + 1) * CH, :])
+        slot(tiles + 1, lambda: e_.to_z())
+        slot(tiles + 2, lambda: c_.widen())
+        slot(tiles + 3, lambda: d_.widen())
+        fwd = dft[:2 * CH, CH:]
+        inv = dft[3 * CH:]
+        for c in range(0, nseq * nch, 2):
+            dy = mm(fwd, jnp.concatenate([dsm[g, c * CH:(c + 1) * CH, :], dsm[g, (c + 1) * CH:(c + 2) * CH, :]], axis=1))
+            dyspec[c] = dy[:, :LG]
+            dyspec[c + 1] = dy[:, LG:]
 
         def a_second():
-            back(two)
-            three.add_x()
-            three.start("z")
+            e_.to_next()
+            a_.wait("back_x")
+            full_a[...] = f0[...]
+            b_.wait("back_x")
+            full_b[...] = f1[...]
+            c_.back()
 
         slot(tiles, a_second)
-
-        def b_first():
-            four.add_y()
-            four.start("x")
-            one.wait("back_x")
-
-        slot(tiles + 1, b_first)
-
-        def c_first():
-            widen(two)
-            back(three)
-            four.add_x()
-            four.start("z")
-
-        slot(tiles + 2, c_first)
-
-        def d_second():
-            widen(three)
-
-        slot(tiles + 3, d_second)
+        slot(tiles + 1, lambda: d_.back())
+        slot(tiles + 2, lambda: e_.back())
+        slot(tiles + 3, lambda: e_.widen())
 
         def point(i, _):
             rc = pl.ds(pl.multiple_of(i * 16, 16), 16)
@@ -1037,16 +1104,20 @@
 
         lax.fori_loop(0, CH // 16, point, 0)
         dgain = 0.
-        for c in range(nseq * nch):
-            r = slice(c * CH, (c + 1) * CH)
-            t = mm_tn(fwd, dxspec[c]) + dn[g, r, :].astype(f32)
-            dn_o[0, r, :] = t.astype(bf)
-            dgain = dgain + jnp.sum((t * xr[g, r, :].astype(f32)).reshape(CH // 8, 8, LG), axis=0)
-        for d in range(nch):
-            dk = mm_tn(fwd, gspec[d])
-            if d + 1 < nch:
-                dk = dk + mm_tn(dft[:, :CH], gspec[d + 1])
-            dkscr[d * CH:(d + 1) * CH, :] = dk * (1.0 / CH)
+        for c in range(0, nseq * nch, 2):
+            both = mm(inv, jnp.concatenate([dxspec[c], dxspec[c + 1]], axis=1))
+            for i in range(2):
+                r = slice((c + i) * CH, (c + i + 1) * CH)
+                t = both[:, i * LG:(i + 1) * LG] + dn[g, r, :].astype(f32)
+                dn_o[0, r, :] = t.astype(bf)
+                dgain = dgain + jnp.sum((t * xr[g, r, :].astype(f32)).reshape(CH // 8, 8, LG), axis=0)
+        whole = dft[2 * CH:]
+        for d in range(0, nch, 2):
+            dk = mm(whole, jnp.concatenate([gspec[d], gspec[d + 1]], axis=1)) * (1.0 / CH)
+            if d:
+                dkscr[(d - 1) * CH:d * CH, :] += dk[:CH, :LG]
+            dkscr[d * CH:(d + 1) * CH, :] = dk[CH:, :LG] + dk[:CH, LG:]
+            dkscr[(d + 1) * CH:(d + 2) * CH, :] = dk[CH:, LG:]
         p = [small[g, i * NH:(i + 1) * NH, :] for i in range(4)]
         a, gg, ex, ro, keep = ema_rates(p)
         p8 = power_of(keep, 8)
@@ -1061,7 +1132,7 @@
 
         none = dkscr[0:8, :] * 0.0
         zero = (none,) * NH
-        A, B = lax.fori_loop(0, seqlen // 8, horner, (zero, zero), unroll=2)
+        A, B = lax.fori_loop(0, seqlen // 8, horner, (zero, zero), unroll=8)
         rr = lax.broadcasted_iota(jnp.int32, (8, LG), 0).astype(f32)
         As = []
         Bs = []
@@ -1078,12 +1149,11 @@
         grads = (da * a * (1.0 - a), dg * gg * (1.0 - gg), a * ro * As, a * ex * As)
         for i, v in enumerate(grads):
             if remote:
-                sums[g, i * NH:(i + 1) * NH, :] = v
+                sums[g, i * NH:(i + 1) * NH, :] = v.astype(bf)
             else:
                 dema_o[i] = v
         if remote:
-            sums[g, 4 * NH:, :] = jnp.concatenate(
-                [jnp.sum(dgain, axis=0, keepdims=True), jnp.zeros((7, LG), f32)], axis=0)
+            gains[g, 0:1, :] = jnp.sum(dgain, axis=0, keepdims=True)
         else:
             dgain_o[...] = dgain
 
@@ -1097,29 +1167,32 @@
         g1 = jnp.sum(gain1[...], axis=0, keepdims=True)
         cols = jnp.sum(aff[...], axis=1)
         for q in range(ng):
-            sums[q, 4 * NH + 1:4 * NH + 6, :] = jnp.concatenate([g1[:, q * LG:(q + 1) * LG], cols], axis=0)
+            sums[q, 4 * NH:, :] = jnp.concatenate(
+                [gains[q, 0:1, :], g1[:, q * LG:(q + 1) * LG], cols, jnp.zeros((SMALL - 4 * NH - 6, LG), f32)],
+                axis=0).astype(bf)
         first = [across(k, sums.at[peer[1]], near.at[k], peer) for k, peer in enumerate(fsdp_peers())]
         for c in first:
             c.start()
-        widen(four)
-        full1[...] = f1[...]
-        full2[...] = f2[...]
         for c in first:
             c.wait()
-        total[...] = sums[fs] + near[0] + near[1] + near[2]
+        t = sums[fs].astype(f32)
+        for k in range(3):
+            t = t + near[k].astype(f32)
+        total[...] = t.astype(bf)
         second = [across(3 + k, total, far.at[k], peer) for k, peer in enumerate(dp_peers())]
         for c in second:
             c.start()
-        three.wait("back_x")
-        full3[...] = f3[...]
+        c_.wait("back_x")
+        full_c[...] = f2[...]
+        d_.wait("back_x")
+        full_d[...] = f3[...]
         for c in second:
             c.wait()
-        t = total[...]
         for k in range(7):
-            t = t + far[k]
+            t = t + far[k].astype(f32)
         small_o[...] = t
-        four.wait("back_x")
-        full4[...] = f4[...]
+        e_.wait("back_x")
+        full_e[...] = f4[...]
 
     slot(tiles + ng - 1, close)
 
@@ -1149,21 +1222,21 @@
     params = {}
     qs = ()
     if remote:
-        piece1, sum2, sum3, keep4, give4, gain1, aff = comm_in
-        n = [piece1.shape[0] * 8, sum2.shape[0], sum3.shape[1], keep4.shape[1]]
+        half_a, piece_b, near_c, near_d, keep_e, *_ = comm_in
+        n = [half_a.shape[0] * 2, piece_b.shape[0] * 8, near_c.shape[0], near_d.shape[1] * 2, keep_e.shape[1]]
         qs = [a // 8 for a in n]
         ins += [(a, const_spec(a)) for a in comm_in]
         fulls = [jax.ShapeDtypeStruct((a, LG), bf) for a in n]
-        one = jax.ShapeDtypeStruct((SMALL, LG), f32)
-        outs += [(a, const_spec(a)) for a in fulls + [one]]
+        one = jax.ShapeDtypeStruct((SMALL, LG), bf)
+        outs += [(a, const_spec(a)) for a in fulls + [jax.ShapeDtypeStruct(one.shape, f32)]]
         v = lambda *s: pltpu.VMEM(s + (LG,), bf)
-        w = lambda *s: pltpu.VMEM(s + one.shape, f32)
-        sem = pltpu.SemaphoreType.DMA((10,))
-        scratch += [v(n[0]), sem, sem,
-                    v(n[1] // 2), v(3, qs[1]), v(n[1]), sem, sem,
-                    v(n[2]), v(n[2] // 2), v(3, qs[2]), v(n[2]), sem, sem,
-                    v(2, n[3]), v(n[3]), v(n[3] // 2), v(3, qs[3]), v(n[3]), sem, sem,
-                    w(4), w(3), w(), w(7), sem, sem]
+        w = lambda *s: pltpu.VMEM(s + one.shape, bf)
+        sem = pltpu.SemaphoreType.DMA((11,))
+        scratch += [v(n[0]), sem, sem, v(n[1]), sem, sem,
+                    v(n[2] // 2), v(3, qs[2]), v(n[2]), sem, sem,
+                    v(n[3] // 2), v(3, qs[3]), v(n[3]), sem, sem,
+                    v(2, n[4]), v(n[4]), v(n[4] // 2), v(3, qs[4]), v(n[4]), sem, sem,
+                    w(4), w(3), w(), w(7), sem, sem, pltpu.VMEM((ng, 8, LG), f32)]
         params = dict(collective_id=3, has_side_effects=True)
     else:
         outs += [(jax.ShapeDtypeStruct((4, NH, D), f32), pl.BlockSpec((4, NH, LG), lambda i: (0, 0, lanes(i)))),
@@ -1203,24 +1276,29 @@
             for q in range(4):
                 mine = mine + jnp.where(fs[0] == q, 1.0, 0.0) * t[4 * NH + 2:4 * NH + 6, q * width:(q + 1) * width]
             aff_o[...] = mine
-            at = 3
-            for full, count in zip(fulls, groups):
+
+        at = 3
+        for i, (full, count) in enumerate(zip(fulls, groups)):
+            @pl.when(pl.program_id(0) == i % 2)
+            def _(full=full, at=at, count=count):
                 unpack(full, outs[at:at + count])
-                at += count
+            at += count
 
 
 def finish_main(fs, tokens, dxd, dn, small, fulls=(), sums=None, groups=(), shapes=()):
     rows, D = tokens.shape
     ng = dn.shape[0]
-    ds = row_spec(D)
+    tile = min(2 * RT, rows)
+    ds = pl.BlockSpec((tile, D), lambda i: (i, 0))
     extra = list(fulls) + ([sums] if groups else [])
     outs = [jax.ShapeDtypeStruct(s, f32) for s in shapes]
     return pl.pallas_call(
         functools.partial(finish_kernel, groups),
-        grid=(rows // RT,),
-        in_specs=[SMEM, ds, ds, pl.BlockSpec((ng, RT, LG), lambda i: (0, i, 0))] + [const_spec(a) for a in [small] + extra],
+        grid=(rows // tile,),
+        in_specs=[SMEM, ds, ds, pl.BlockSpec((ng, tile, LG), lambda i: (0, i, 0))] + [const_spec(a) for a in [small] + extra],
         out_specs=[ds] + [const_spec(a) for a in outs],
         out_shape=[jax.ShapeDtypeStruct((rows, D), bf)] + outs,
+        compiler_params=pltpu.CompilerParams(vmem_limit_bytes=60 * 2**20),
         name="finish",
     )(fs, tokens, dxd, dn, small, *extra)
 
@@ -1252,9 +1330,9 @@
         return output, grad_tokens, (grad_gains, jnp.swapaxes(g_ema, 1, 2), jnp.sum(g_aff, axis=1), *second, *first)
     dn, *fulls, sums = input_main(*shared, (*second, g_gain1, g_aff))
     shapes = [norm_gains.shape, ema_t.shape, qk_affine.shape]
-    shapes += [w.shape for w in (w_in, w_out, w_h, u_h, w_u, w_r, w_v, w_z)]
-    grad_tokens, g_gains, g_ema, g_aff, g_in, g_out, g_h, g_uh, g_u, g_r, g_v, g_z = finish_main(
-        fs, tokens, dxd, dn, small, fulls, sums, (2, 3, 1, 2), shapes)
+    shapes += [w.shape for w in (w_out, w_in, w_r, w_h, u_h, w_u, w_v, w_z)]
+    grad_tokens, g_gains, g_ema, g_aff, g_out, g_in, g_r, g_h, g_uh, g_u, g_v, g_z = finish_main(
+        fs, tokens, dxd, dn, small, fulls, sums, (1, 1, 2, 2, 2), shapes)
     return output, grad_tokens, (g_gains, jnp.swapaxes(g_ema, 1, 2), g_aff, g_z, g_v, g_r, g_u, g_h, g_uh, g_in, g_out)
 
 

time: 192 us -> 177 us (0.922)
  Pallas kernels: 191 us -> 176 us
    pallas_call x1, Pallas kernels: 60 us -> 52.4 us  [input_main(): pl.pallas_call(functools.partial(input_kernel, nseq, seqlen, qs, remote),...]
    pallas_call x1, Pallas kernels: 44.4 us -> 41.3 us  [backward_main(): pl.pallas_call(functools.partial(backward_kernel, qs, remote), grid=(2 *...]
    pallas_call x1, Pallas kernels: 28.2 us -> 26.2 us  [forward_main(): pl.pallas_call(functools.partial(forward_kernel, rows // nseq, remote), g...]
where the time goes in v2:
time: 177 us
  Pallas kernels  176 us (99%)
    pallas_call x1, Pallas kernels, input_main(): pl.pallas_call(functools.partial(input_kernel, nseq, seqlen, qs, remote),...  52.4 us
    pallas_call x1, Pallas kernels, backward_main(): pl.pallas_call(functools.partial(backward_kernel, qs, remote), grid=(2 *...  41.3 us
    pallas_call x1, Pallas kernels, ema_forward(): pl.pallas_call(functools.partial(ema_fwd_kernel, nseq, seqlen, remote), g...  29.2 us
    pallas_call x1, Pallas kernels, forward_main(): pl.pallas_call(functools.partial(forward_kernel, rows // nseq, remote), g...  26.2 us
    pallas_call x1, Pallas kernels, ffn_main(): pl.pallas_call(functools.partial(ffn_kernel, packed), grid=(rows // TT,),...  20.3 us
    pallas_call x1, Pallas kernels, finish_main(): pl.pallas_call(functools.partial(finish_kernel, groups), grid=(rows // ti...  6.79 us

profile of v2, /device:TPU:0, one launch (start us, length us, event | category | flops | bytes accessed | tf_op | source)
XLA Modules:
  0.0 176.9 jit_solution(142745023675437252)
XLA Ops:
  0.7 29.2 %ema_fwd.1 = (bf16[2048,512]{1,0:T(8,128)(2,1)}, bf16[2048,512]{1,0:T(8,128)(2,1)}, bf16[8,512,512]{2,1,0:T(8,128)(2,1)}, bf16[4,512,512]{2,1,0:T(8,128)(2,1)}, ...) custom-call(bf16[2048,512]{1,0:T(8,128)(2,1)} %tok.7, ...), custom_call_target="tpu_custom_call" | custom-call | tf_op jit(solution)/shard_map/ema_fwd/pallas_call | solution.py:350
  29.8 26.2 %forward_main.1 = (bf16[2048,512]{1,0:T(8,128)(2,1)}, bf16[2048,512]{1,0:T(8,128)(2,1)}, bf16[2048,512]{1,0:T(8,128)(2,1)}, bf16[2048,512]{1,0:T(8,128)(2,1)}, b...) custom-call(s32[2]{0:T(128)} %lens.1, ...), custom_call_target="tpu_custom_call" | custom-call | tf_op jit(solution)/shard_map/forward_main/pallas_call | solution.py:677
  56.0 20.3 %ffn_main.1 = (bf16[2048,512]{1,0:T(8,128)(2,1)}, bf16[2048,512]{1,0:T(8,128)(2,1)}, f32[8,512]{1,0:T(8,128)}, bf16[2,1024,128]{2,1,0:T(8,128)(2,1)}, bf16[2,102...) custom-call(s32[1]{0:T(128)} %bitcast.fs, ...), custom_call_target="tpu_custom_call" | custom-call | tf_op jit(solution)/shard_map/ffn_main/pallas_call | solution.py:745
  76.3 41.3 %backward_main.1 = (bf16[2048,512]{1,0:T(8,128)(2,1)}, bf16[2048,512]{1,0:T(8,128)(2,1)}, bf16[2048,512]{1,0:T(8,128)(2,1)}, bf16[2048,1024]{1,0:T(8,128)(2,1)},...) custom-call(bf16[2048,512]{1,0:T(8,128)(2,1)} %get-tuple-element.83., ...), custom_call_target="tpu_custom_call" | custom-call | tf_op jit(solution)/shard_map/backward_main/pallas_call | solution.py:955
  117.5 52.4 %input_main.1 = (bf16[4,2048,128]{2,1,0:T(8,128)(2,1)}, bf16[1024,128]{1,0:T(8,128)(2,1)}, bf16[1024,128]{1,0:T(8,128)(2,1)}, bf16[1536,128]{1,0:T(8,128)(2,1)},...) custom-call(bf16[2048,512]{1,0:T(8,128)(2,1)} %get-tuple-element.99.gh, ...), custom_call_target="tpu_custom_call" | custom-call | tf_op jit(solution)/shard_map/input_main/pallas_call | solution.py:1244
  169.9 6.8 %finish.1 = (bf16[2048,512]{1,0:T(8,128)(2,1)}, f32[2,128]{1,0:T(2,128)}, f32[4,16,128]{2,1,0:T(8,128)}, f32[4,32]{1,0:T(4,128)}, f32[256,512]{1,0:T(8,128)}, /*...) custom-call(s32[1]{0:T(128)} %bitcast.fs, ...), custom_call_target="tpu_custom_call" | custom-call | tf_op jit(solution)/shard_map/finish/pallas_call | solution.py:1295

commit v3 on v2

--- a/solution.py
+++ b/solution.py
@@ -242,13 +242,7 @@
     slot(0, settle)
 
     slot(1, lambda: gather.relay(1))
-    slot(2, lambda: gather.cross(1))
-
-    def last_first():
-        gather.last(0)
-        gather.last(1)
-
-    slot(3, last_first)
+    slot(2, lambda: gather.cross(0))
     p = [small[g, i * NH:(i + 1) * NH, :] for i in range(4)]
     normed = (nscr[g] * small[g, 4 * NH:4 * NH + 1, :]).astype(bf)
     normed_o[...] = normed
@@ -286,7 +280,8 @@
             xs_o[c + i] = xd[:, i * LG:(i + 1) * LG].astype(bf)
 
     slot(1, lambda: gather.relay(2))
-    slot(2, lambda: gather.cross(2))
+    slot(2, lambda: gather.cross(1))
+    slot(3, lambda: gather.last(0))
 
     def point(i, _):
         rc = pl.ds(pl.multiple_of(i * 16, 16), 16)
@@ -308,7 +303,8 @@
 
     lax.fori_loop(0, CH // 16, point, 0)
     slot(0, lambda: gather.relay(0))
-    slot(1, lambda: gather.cross(0))
+    slot(2, lambda: gather.cross(2))
+    slot(3, lambda: gather.last(1))
     for c in range(0, nseq * nch, 2):
         y = mm(inv, jnp.concatenate([yspec[c], yspec[c + 1]], axis=1)).astype(bf)
         smooth_o[c * CH:(c + 1) * CH, :] = y[:, :LG]
@@ -445,10 +441,13 @@
         self.add_near()
         self.start("next")
 
-    def to_z(self):
+    def add_next(self):
         self.wait("next")
         src = self.near.at[self.half(self.x)] if self.first == "y" else self.near.at[self.y]
         self.add(self.mid, src, 4 * self.q)
+
+    def to_z(self):
+        self.add_next()
         self.start("z")
 
     def add_z(self):
@@ -720,7 +719,9 @@
         gwi[:, c] += mm_tn(y, gf)
     out_o[...] = (m + mm(ascr[...], w_out[...])).astype(bf)
     dy = mm_nt(gscr[...], w_in[...])
-    dg_o[...] += jnp.sum((dy * mr).reshape(TT // 8, 8, m.shape[1]), axis=0)
+    part = jnp.sum((dy * mr).reshape(TT // 8, 8, m.shape[1]), axis=0)
+    for j in range(m.shape[1] // LG):
+        dg_o[j] += part[:, j * LG:(j + 1) * LG]
     dyg = dy * gn
     inner = jnp.mean(dyg * mr, axis=-1, keepdims=True)
     dm_o[...] = (cl.astype(f32) + inv * (dyg - mr * inner)).astype(bf)
@@ -741,7 +742,7 @@
     accs = [(D, ff), (ff, D)]
     pair = [jax.ShapeDtypeStruct((2, D * ff // 4 // LG, LG), bf)] * 4
     extra = pair if packed else [jax.ShapeDtypeStruct(s, f32) for s in accs]
-    gain = jax.ShapeDtypeStruct((8, D), f32)
+    gain = jax.ShapeDtypeStruct((D // LG, 8, LG), f32)
     return pl.pallas_call(
         functools.partial(ffn_kernel, packed),
         grid=(rows // TT,),
@@ -993,7 +994,7 @@
         mid2, z2, f2, s2, r2 = take(5)
         mid3, z3, f3, s3, r3 = take(5)
         core4, near4, mid4, z4, f4, s4, r4 = take(7)
-        sums, near, total, far, s5, r5, gains = take(7)
+        sums, near, total, far, s5, r5 = take(6)
         a_ = Reduce(qs[0], "y", s0, r0, full=f0)
         b_ = Reduce(qs[1], "x", s1, r1, full=f1)
         c_ = Reduce(qs[2], "y", s2, r2, near=near_c, mid=mid2, z_in=z2, full=f2)
@@ -1003,6 +1004,20 @@
     def slot(at, fn):
         if remote:
             pl.when(step == at)(fn)
+
+    if remote:
+        fs = lax.axis_index("fsdp")
+
+    def across(k, src, dst, peer):
+        return pltpu.make_async_remote_copy(src_ref=src, dst_ref=dst, send_sem=s5.at[k], recv_sem=r5.at[k],
+                                            device_id=peer, device_id_type=MESH)
+
+    def gathered():
+        return [across(k, sums.at[peer[1]], near.at[k], peer) for k, peer in enumerate(fsdp_peers())]
+
+    def hand_over(block):
+        for copy, peer in zip(gathered(), fsdp_peers()):
+            pl.when(peer[1] == block)(copy.start)
 
     def open_up():
         greet(fsdp_peers() + dp_peers())
@@ -1022,11 +1037,8 @@
 
     slot(1, at_one)
 
-    def at_two():
+    def at_three():
         c_.to_z()
-
-    slot(2, at_two)
-    def at_three():
         d_.to_z()
         b_.widen()
 
@@ -1048,11 +1060,17 @@
 
     @pl.when(step >= tiles)
     def _():
-        g = step - tiles
-
-        slot(tiles + 1, lambda: e_.to_z())
-        slot(tiles + 2, lambda: c_.widen())
-        slot(tiles + 3, lambda: d_.widen())
+        g = lax.rem(step - tiles + 1 + fs, ng) if remote else step - tiles
+
+        if remote:
+            @pl.when(step > tiles)
+            def _():
+                hand_over(lax.rem(step - tiles + fs, ng))
+
+
+        slot(tiles, lambda: e_.to_next())
+        slot(tiles + 2, lambda: d_.back())
+        slot(tiles + 3, lambda: c_.widen())
         fwd = dft[:2 * CH, CH:]
         inv = dft[3 * CH:]
         for c in range(0, nseq * nch, 2):
@@ -1061,17 +1079,19 @@
             dyspec[c + 1] = dy[:, LG:]
 
         def a_second():
-            e_.to_next()
             a_.wait("back_x")
             full_a[...] = f0[...]
+
+        slot(tiles, a_second)
+
+        def b_second():
+            c_.back()
+            e_.to_z()
             b_.wait("back_x")
             full_b[...] = f1[...]
-            c_.back()
-
-        slot(tiles, a_second)
-        slot(tiles + 1, lambda: d_.back())
-        slot(tiles + 2, lambda: e_.back())
-        slot(tiles + 3, lambda: e_.widen())
+
+        slot(tiles + 1, b_second)
+        slot(tiles + 3, lambda: e_.back())
 
         def point(i, _):
             rc = pl.ds(pl.multiple_of(i * 16, 16), 16)
@@ -1153,27 +1173,15 @@
             else:
                 dema_o[i] = v
         if remote:
-            gains[g, 0:1, :] = jnp.sum(dgain, axis=0, keepdims=True)
+            lead = [jnp.sum(dgain, axis=0, keepdims=True), jnp.sum(gain1[g], axis=0, keepdims=True)]
+            pad = jnp.zeros((SMALL - 4 * NH - 6, LG), f32)
+            sums[g, 4 * NH:, :] = jnp.concatenate(lead + [jnp.sum(aff[...], axis=1), pad], axis=0).astype(bf)
         else:
             dgain_o[...] = dgain
 
     def close():
-        fs = lax.axis_index("fsdp")
-
-        def across(k, src, dst, peer):
-            return pltpu.make_async_remote_copy(src_ref=src, dst_ref=dst, send_sem=s5.at[k], recv_sem=r5.at[k],
-                                                device_id=peer, device_id_type=MESH)
-
-        g1 = jnp.sum(gain1[...], axis=0, keepdims=True)
-        cols = jnp.sum(aff[...], axis=1)
-        for q in range(ng):
-            sums[q, 4 * NH:, :] = jnp.concatenate(
-                [gains[q, 0:1, :], g1[:, q * LG:(q + 1) * LG], cols, jnp.zeros((SMALL - 4 * NH - 6, LG), f32)],
-                axis=0).astype(bf)
-        first = [across(k, sums.at[peer[1]], near.at[k], peer) for k, peer in enumerate(fsdp_peers())]
-        for c in first:
-            c.start()
-        for c in first:
+        d_.widen()
+        for c in gathered():
             c.wait()
         t = sums[fs].astype(f32)
         for k in range(3):
@@ -1182,15 +1190,16 @@
         second = [across(3 + k, total, far.at[k], peer) for k, peer in enumerate(dp_peers())]
         for c in second:
             c.start()
+        e_.widen()
         c_.wait("back_x")
         full_c[...] = f2[...]
-        d_.wait("back_x")
-        full_d[...] = f3[...]
         for c in second:
             c.wait()
         for k in range(7):
             t = t + far[k].astype(f32)
         small_o[...] = t
+        d_.wait("back_x")
+        full_d[...] = f3[...]
         e_.wait("back_x")
         full_e[...] = f4[...]
 
@@ -1210,7 +1219,8 @@
         return pl.BlockSpec((RT, a.shape[1]), lambda i: (jnp.minimum(i, tiles - 1), 0))
 
     def lanes(i):
-        return jnp.maximum(i - tiles, 0)
+        at = jnp.maximum(i - tiles, 0)
+        return lax.rem(at + 1 + lax.axis_index("fsdp"), ng) if remote else at
 
     ins = [(a, early(a)) for a in grads] + [(w_a, const_spec(w_a)), (tokens, early(tokens)), (small, const_spec(small))]
     ins += [(dft, const_spec(dft)), (xspec, pl.BlockSpec((nchunks, 2 * CH, LG), lambda i: (0, 0, lanes(i)))),
@@ -1236,7 +1246,7 @@
                     v(n[2] // 2), v(3, qs[2]), v(n[2]), sem, sem,
                     v(n[3] // 2), v(3, qs[3]), v(n[3]), sem, sem,
                     v(2, n[4]), v(n[4]), v(n[4] // 2), v(3, qs[4]), v(n[4]), sem, sem,
-                    w(4), w(3), w(), w(7), sem, sem, pltpu.VMEM((ng, 8, LG), f32)]
+                    w(4), w(3), w(), w(7), sem, sem]
         params = dict(collective_id=3, has_side_effects=True)
     else:
         outs += [(jax.ShapeDtypeStruct((4, NH, D), f32), pl.BlockSpec((4, NH, LG), lambda i: (0, 0, lanes(i)))),
@@ -1326,7 +1336,7 @@
     if not remote:
         dn, g_ema, g_gain0 = input_main(*shared)
         grad_tokens, = finish_main(fs, tokens, dxd, dn, small)
-        grad_gains = jnp.stack([jnp.sum(g_gain0, axis=0), jnp.sum(g_gain1, axis=0)])
+        grad_gains = jnp.stack([jnp.sum(g_gain0, axis=0), jnp.sum(g_gain1, axis=1).reshape(D)])
         return output, grad_tokens, (grad_gains, jnp.swapaxes(g_ema, 1, 2), jnp.sum(g_aff, axis=1), *second, *first)
     dn, *fulls, sums = input_main(*shared, (*second, g_gain1, g_aff))
     shapes = [norm_gains.shape, ema_t.shape, qk_affine.shape]

time: 177 us -> 173 us (0.977)
  Pallas kernels: 176 us -> 172 us
    pallas_call x1, Pallas kernels: 52.4 us -> 49.8 us  [input_main(): pl.pallas_call(functools.partial(input_kernel, nseq, seqlen, qs, remote),...]
where the time goes in v3:
time: 173 us
  Pallas kernels  172 us (99%)
    pallas_call x1, Pallas kernels, input_main(): pl.pallas_call(functools.partial(input_kernel, nseq, seqlen, qs, remote),...  49.8 us
    pallas_call x1, Pallas kernels, backward_main(): pl.pallas_call(functools.partial(backward_kernel, qs, remote), grid=(2 *...  41.3 us
    pallas_call x1, Pallas kernels, ema_forward(): pl.pallas_call(functools.partial(ema_fwd_kernel, nseq, seqlen, remote), g...  27.9 us
    pallas_call x1, Pallas kernels, forward_main(): pl.pallas_call(functools.partial(forward_kernel, rows // nseq, remote), g...  25.9 us
    pallas_call x1, Pallas kernels, ffn_main(): pl.pallas_call(functools.partial(ffn_kernel, packed), grid=(rows // TT,),...  20.3 us
    pallas_call x1, Pallas kernels, finish_main(): pl.pallas_call(functools.partial(finish_kernel, groups), grid=(rows // ti...  6.79 us

profile of v3, /device:TPU:0, one launch (start us, length us, event | category | flops | bytes accessed | tf_op | source)
XLA Modules:
  0.0 172.8 jit_solution(10091302769596716924)
XLA Ops:
  0.7 27.9 %ema_fwd.1 = (bf16[2048,512]{1,0:T(8,128)(2,1)}, bf16[2048,512]{1,0:T(8,128)(2,1)}, bf16[8,512,512]{2,1,0:T(8,128)(2,1)}, bf16[4,512,512]{2,1,0:T(8,128)(2,1)}, ...) custom-call(bf16[2048,512]{1,0:T(8,128)(2,1)} %tok.7, ...), custom_call_target="tpu_custom_call" | custom-call | tf_op jit(solution)/shard_map/ema_fwd/pallas_call | solution.py:346
  28.6 25.9 %forward_main.1 = (bf16[2048,512]{1,0:T(8,128)(2,1)}, bf16[2048,512]{1,0:T(8,128)(2,1)}, bf16[2048,512]{1,0:T(8,128)(2,1)}, bf16[2048,512]{1,0:T(8,128)(2,1)}, b...) custom-call(s32[2]{0:T(128)} %lens.1, ...), custom_call_target="tpu_custom_call" | custom-call | tf_op jit(solution)/shard_map/forward_main/pallas_call | solution.py:676
  54.5 20.3 %ffn_main.1 = (bf16[2048,512]{1,0:T(8,128)(2,1)}, bf16[2048,512]{1,0:T(8,128)(2,1)}, f32[4,8,128]{2,1,0:T(8,128)}, bf16[2,1024,128]{2,1,0:T(8,128)(2,1)}, bf16[2...) custom-call(s32[1]{0:T(128)} %bitcast.fs, ...), custom_call_target="tpu_custom_call" | custom-call | tf_op jit(solution)/shard_map/ffn_main/pallas_call | solution.py:746
  74.8 41.3 %backward_main.1 = (bf16[2048,512]{1,0:T(8,128)(2,1)}, bf16[2048,512]{1,0:T(8,128)(2,1)}, bf16[2048,512]{1,0:T(8,128)(2,1)}, bf16[2048,1024]{1,0:T(8,128)(2,1)},...) custom-call(bf16[2048,512]{1,0:T(8,128)(2,1)} %get-tuple-element.83., ...), custom_call_target="tpu_custom_call" | custom-call | tf_op jit(solution)/shard_map/backward_main/pallas_call | solution.py:956
  116.1 49.8 %input_main.1 = (bf16[4,2048,128]{2,1,0:T(8,128)(2,1)}, bf16[1024,128]{1,0:T(8,128)(2,1)}, bf16[1024,128]{1,0:T(8,128)(2,1)}, bf16[1536,128]{1,0:T(8,128)(2,1)},...) custom-call(bf16[2048,512]{1,0:T(8,128)(2,1)} %get-tuple-element.99.gh, ...), custom_call_target="tpu_custom_call" | custom-call | tf_op jit(solution)/shard_map/input_main/pallas_call | solution.py:1254
  165.8 6.8 %finish.1 = (bf16[2048,512]{1,0:T(8,128)(2,1)}, f32[2,128]{1,0:T(2,128)}, f32[4,16,128]{2,1,0:T(8,128)}, f32[4,32]{1,0:T(4,128)}, f32[256,512]{1,0:T(8,128)}, /*...) custom-call(s32[1]{0:T(128)} %bitcast.fs, ...), custom_call_target="tpu_custom_call" | custom-call | tf_op jit(solution)/shard_map/finish/pallas_call | solution.py:1305

commit v4 on v3

--- a/solution.py
+++ b/solution.py
@@ -68,9 +68,9 @@
 
 
 class Gather:
-    def __init__(self, shards, outs, pieces, send, recv, local):
+    def __init__(self, shards, outs, pieces, send, recv, local, straight=()):
         self.shards, self.outs, self.pieces = shards, outs, pieces
-        self.send, self.recv, self.local = send, recv, local
+        self.send, self.recv, self.local, self.straight = send, recv, local, straight
         self.dp = lax.axis_index("dp")
         self.fs = lax.axis_index("fsdp")
         self.x = self.dp % 2
@@ -79,6 +79,9 @@
         self.y_peer = (self.dp, flip(self.fs, 2))
         self.x_peer = (flip(self.dp, 1), self.fs)
         self.z_peer = (flip(self.dp, 2), self.fs)
+
+        self.x_across = (self.x_peer[0], self.core_peer[1])
+        self.z_across = (self.z_peer[0], self.core_peer[1])
 
     def peers(self):
         return [self.core_peer, self.y_peer, self.x_peer, self.z_peer]
@@ -106,14 +109,16 @@
             (at(out, far, z, 1 - x),) * 2 + (self.core_peer,),
             (at(out, far, 1 - z, x),) * 2 + (self.core_peer,),
             (at(out, far, 1 - z, 1 - x),) * 2 + (self.core_peer,),
+            (at(out, far, 1 - z, x, 0),) * 2 + (self.x_across,),
+            (at(out, far, z, 1 - x, 1),) * 2 + (self.z_across,),
         )[k]
         return pltpu.make_async_remote_copy(
-            src_ref=src, dst_ref=dst, send_sem=self.send.at[9 * p + k], recv_sem=self.recv.at[9 * p + k],
+            src_ref=src, dst_ref=dst, send_sem=self.send.at[11 * p + k], recv_sem=self.recv.at[11 * p + k],
             device_id=peer, device_id_type=MESH)
 
     def whole(self, a):
         n = self.shards[a].shape[0]
-        slot = 9 * len(self.pieces) + a
+        slot = 11 * len(self.pieces) + a
         return pltpu.make_async_remote_copy(
             src_ref=self.shards[a], dst_ref=self.outs[a].at[pl.ds(pl.multiple_of(self.fs * n, n), n)],
             send_sem=self.send.at[slot], recv_sem=self.recv.at[slot], device_id=self.core_peer, device_id_type=MESH)
@@ -136,23 +141,26 @@
             self.copy(p, k).start()
 
     def cross(self, p):
+        straight = p in self.straight
         self.copy(p, 2).wait_recv()
-        self.copy(p, 3).start()
-        self.copy(p, 7).start()
+        for k in (3, 9, 7) if straight else (3, 7):
+            self.copy(p, k).start()
         self.copy(p, 1).wait_recv()
-        self.copy(p, 4).start()
-        self.copy(p, 6).start()
+        for k in (4, 10, 6) if straight else (4, 6):
+            self.copy(p, k).start()
 
     def last(self, p):
         self.copy(p, 3).wait_recv()
         self.copy(p, 4).wait_recv()
-        self.copy(p, 8).start()
+        if p not in self.straight:
+            self.copy(p, 8).start()
 
     def finish(self):
         for p in range(len(self.pieces)):
-            for k in range(9):
+            ends = (9, 10) if p in self.straight else (8,)
+            for k in (0, 1, 2, 3, 4, 5, 6, 7) + ends:
                 self.copy(p, k).wait_send()
-            for k in (5, 6, 7, 8):
+            for k in (5, 6, 7) + ends:
                 self.copy(p, k).wait_recv()
         for a in range(len(self.shards)):
             self.whole(a).wait()
@@ -160,7 +168,7 @@
 
 
 def gather_sems(arrays, pieces):
-    sem = pltpu.SemaphoreType.DMA((9 * pieces + arrays,))
+    sem = pltpu.SemaphoreType.DMA((11 * pieces + arrays,))
     return [sem, sem, pltpu.SemaphoreType.DMA((arrays,))]
 
 
@@ -191,7 +199,7 @@
         small, sent, own, s1, r1, *sems = take(8)
         fs = lax.axis_index("fsdp")
         gather = Gather((own, parts[5]), (w_full, u_full),
-                        ((0, 0, 1664), (0, 1664, own.shape[1] - 1664), (1, 0, parts[5].shape[1])), *sems)
+                        ((0, 0, 1664), (0, 1664, own.shape[1] - 1664), (1, 0, parts[5].shape[1])), *sems, (2,))
         across = [pltpu.make_async_remote_copy(
             src_ref=sent.at[fs], dst_ref=sent.at[fs], send_sem=s1.at[k], recv_sem=r1.at[k],
             device_id=peer, device_id_type=MESH) for k, peer in enumerate(fsdp_peers())]
@@ -201,7 +209,7 @@
             pl.when(g == at)(fn)
 
     def open_up():
-        greet(fsdp_peers() + [gather.x_peer, gather.z_peer])
+        greet(fsdp_peers() + [gather.x_peer, gather.z_peer, gather.x_across, gather.z_across])
         for i in range(4):
             sent[fs, i * NH:(i + 1) * NH, :] = ema_i[i]
         tail = [gain_i[...].astype(f32), jnp.concatenate([aff_i[...].astype(f32)] * 4, axis=1),
@@ -211,7 +219,7 @@
         for w in parts[:5]:
             own[:, at:at + w.shape[1]] = w[...]
             at += w.shape[1]
-        met(5)
+        met(7)
         for c in across:
             c.start()
         gather.begin()
@@ -241,8 +249,6 @@
 
     slot(0, settle)
 
-    slot(1, lambda: gather.relay(1))
-    slot(2, lambda: gather.cross(0))
     p = [small[g, i * NH:(i + 1) * NH, :] for i in range(4)]
     normed = (nscr[g] * small[g, 4 * NH:4 * NH + 1, :]).astype(bf)
     normed_o[...] = normed
@@ -265,6 +271,9 @@
 
     lax.fori_loop(0, seqlen // 16, kgen, tuple(z0), unroll=4)
     kscr[0:CH, :] = jnp.zeros((CH, LG), bf)
+    slot(1, lambda: gather.relay(1))
+    slot(2, lambda: gather.cross(0))
+    slot(3, lambda: gather.cross(2))
     both = dft[:2 * CH]
     fwd = dft[:2 * CH, CH:]
     inv = dft[3 * CH:]
@@ -280,7 +289,6 @@
             xs_o[c + i] = xd[:, i * LG:(i + 1) * LG].astype(bf)
 
     slot(1, lambda: gather.relay(2))
-    slot(2, lambda: gather.cross(1))
     slot(3, lambda: gather.last(0))
 
     def point(i, _):
@@ -303,7 +311,7 @@
 
     lax.fori_loop(0, CH // 16, point, 0)
     slot(0, lambda: gather.relay(0))
-    slot(2, lambda: gather.cross(2))
+    slot(2, lambda: gather.cross(1))
     slot(3, lambda: gather.last(1))
     for c in range(0, nseq * nch, 2):
         y = mm(inv, jnp.concatenate([yspec[c], yspec[c + 1]], axis=1)).astype(bf)
@@ -1069,7 +1077,11 @@
 
 
         slot(tiles, lambda: e_.to_next())
-        slot(tiles + 2, lambda: d_.back())
+        def c_first():
+            e_.to_z()
+            d_.back()
+
+        slot(tiles + 2, c_first)
         slot(tiles + 3, lambda: c_.widen())
         fwd = dft[:2 * CH, CH:]
         inv = dft[3 * CH:]
@@ -1086,7 +1098,6 @@
 
         def b_second():
             c_.back()
-            e_.to_z()
             b_.wait("back_x")
             full_b[...] = f1[...]
 

time: 173 us -> 172 us (level)
  no operation moved by 1% of the time
where the time goes in v4:
time: 172 us
  Pallas kernels  171 us (99%)
    pallas_call x1, Pallas kernels, input_main(): pl.pallas_call(functools.partial(input_kernel, nseq, seqlen, qs, remote),...  49.5 us
    pallas_call x1, Pallas kernels, backward_main(): pl.pallas_call(functools.partial(backward_kernel, qs, remote), grid=(2 *...  41.3 us
    pallas_call x1, Pallas kernels, forward_main(): pl.pallas_call(functools.partial(forward_kernel, rows // nseq, remote), g...  26.5 us
    pallas_call x1, Pallas kernels, ema_forward(): pl.pallas_call(functools.partial(ema_fwd_kernel, nseq, seqlen, remote), g...  26.4 us
    pallas_call x1, Pallas kernels, ffn_main(): pl.pallas_call(functools.partial(ffn_kernel, packed), grid=(rows // TT,),...  20.2 us
    pallas_call x1, Pallas kernels, finish_main(): pl.pallas_call(functools.partial(finish_kernel, groups), grid=(rows // ti...  6.79 us

profile of v4, /device:TPU:0, one launch (start us, length us, event | category | flops | bytes accessed | tf_op | source)
XLA Modules:
  0.0 171.6 jit_solution(95544448420443034)
XLA Ops:
  0.7 26.4 %ema_fwd.1 = (bf16[2048,512]{1,0:T(8,128)(2,1)}, bf16[2048,512]{1,0:T(8,128)(2,1)}, bf16[8,512,512]{2,1,0:T(8,128)(2,1)}, bf16[4,512,512]{2,1,0:T(8,128)(2,1)}, ...) custom-call(bf16[2048,512]{1,0:T(8,128)(2,1)} %tok.7, ...), custom_call_target="tpu_custom_call" | custom-call | tf_op jit(solution)/shard_map/ema_fwd/pallas_call | solution.py:354
  27.1 26.5 %forward_main.1 = (bf16[2048,512]{1,0:T(8,128)(2,1)}, bf16[2048,512]{1,0:T(8,128)(2,1)}, bf16[2048,512]{1,0:T(8,128)(2,1)}, bf16[2048,512]{1,0:T(8,128)(2,1)}, b...) custom-call(s32[2]{0:T(128)} %lens.1, ...), custom_call_target="tpu_custom_call" | custom-call | tf_op jit(solution)/shard_map/forward_main/pallas_call | solution.py:684
  53.5 20.2 %ffn_main.1 = (bf16[2048,512]{1,0:T(8,128)(2,1)}, bf16[2048,512]{1,0:T(8,128)(2,1)}, f32[4,8,128]{2,1,0:T(8,128)}, bf16[2,1024,128]{2,1,0:T(8,128)(2,1)}, bf16[2...) custom-call(s32[1]{0:T(128)} %bitcast.fs, ...), custom_call_target="tpu_custom_call" | custom-call | tf_op jit(solution)/shard_map/ffn_main/pallas_call | solution.py:754
  73.8 41.3 %backward_main.1 = (bf16[2048,512]{1,0:T(8,128)(2,1)}, bf16[2048,512]{1,0:T(8,128)(2,1)}, bf16[2048,512]{1,0:T(8,128)(2,1)}, bf16[2048,1024]{1,0:T(8,128)(2,1)},...) custom-call(bf16[2048,512]{1,0:T(8,128)(2,1)} %get-tuple-element.83., ...), custom_call_target="tpu_custom_call" | custom-call | tf_op jit(solution)/shard_map/backward_main/pallas_call | solution.py:964
  115.1 49.5 %input_main.1 = (bf16[4,2048,128]{2,1,0:T(8,128)(2,1)}, bf16[1024,128]{1,0:T(8,128)(2,1)}, bf16[1024,128]{1,0:T(8,128)(2,1)}, bf16[1536,128]{1,0:T(8,128)(2,1)},...) custom-call(bf16[2048,512]{1,0:T(8,128)(2,1)} %get-tuple-element.99.gh, ...), custom_call_target="tpu_custom_call" | custom-call | tf_op jit(solution)/shard_map/input_main/pallas_call | solution.py:1265
  164.6 6.8 %finish.1 = (bf16[2048,512]{1,0:T(8,128)(2,1)}, f32[2,128]{1,0:T(2,128)}, f32[4,16,128]{2,1,0:T(8,128)}, f32[4,32]{1,0:T(4,128)}, f32[256,512]{1,0:T(8,128)}, /*...) custom-call(s32[1]{0:T(128)} %bitcast.fs, ...), custom_call_target="tpu_custom_call" | custom-call | tf_op jit(solution)/shard_map/finish/pallas_call | solution.py:1316

commit v5 on v4

--- a/solution.py
+++ b/solution.py
@@ -624,26 +624,25 @@
 
     slot(3, last)
     rows = base + lax.broadcasted_iota(jnp.int32, (RT, 1), 0)
-    live = (rows < length).astype(f32)
+    live = (rows < length).astype(f32).astype(bf)
     for j in range(vd // 256):
         c = slice(j * 256, (j + 1) * 256)
-        vp = mm(n, w_v[:, c])
+        vp = mm(n, w_v[:, c]).astype(bf)
         sg = sigm(vp)
         v = vp * sg
-        vl = v.astype(bf)
-        val_o[:, c] = vl
-        vsl_o[:, c] = (sg + v - v * sg).astype(bf)
+        val_o[:, c] = v
+        vsl_o[:, c] = sg + v - v * sg
         att = jnp.concatenate(
-            [mm(probs[b], vl[b * SPAN:(b + 1) * SPAN]) for b in range(RT // SPAN)], axis=0)
-        rp = mm(s, w_r[:, c])
+            [mm(probs[b], v[b * SPAN:(b + 1) * SPAN]) for b in range(RT // SPAN)], axis=0)
+        rp = mm(s, w_r[:, c]).astype(bf)
         sg = sigm(rp)
         re = rp * sg
-        att = att * live
-        ga = (re * att).astype(bf)
+        att = att.astype(bf) * live
+        ga = re * att
         gat_o[:, c] = ga
         gscr[:, c] = ga
-        rv_o[:, c] = (re * live).astype(bf)
-        a2_o[:, c] = (att * (sg + re - re * sg)).astype(bf)
+        rv_o[:, c] = re * live
+        a2_o[:, c] = att * (sg + re - re * sg)
     for j in range(w_h.shape[1] // 256):
         c = slice(j * 256, (j + 1) * 256)
         hp = mm(s, w_h[:, c]) + mm(gscr[...], u_h[:, c])

time: 172 us -> 171 us (level)
  no operation moved by 1% of the time
where the time goes in v5:
time: 171 us
  Pallas kernels  170 us (99%)
    pallas_call x1, Pallas kernels, input_main(): pl.pallas_call(functools.partial(input_kernel, nseq, seqlen, qs, remote),...  49.8 us
    pallas_call x1, Pallas kernels, backward_main(): pl.pallas_call(functools.partial(backward_kernel, qs, remote), grid=(2 *...  41 us
    pallas_call x1, Pallas kernels, ema_forward(): pl.pallas_call(functools.partial(ema_fwd_kernel, nseq, seqlen, remote), g...  26.4 us
    pallas_call x1, Pallas kernels, forward_main(): pl.pallas_call(functools.partial(forward_kernel, rows // nseq, remote), g...  25.8 us
    pallas_call x1, Pallas kernels, ffn_main(): pl.pallas_call(functools.partial(ffn_kernel, packed), grid=(rows // TT,),...  20.3 us
    pallas_call x1, Pallas kernels, finish_main(): pl.pallas_call(functools.partial(finish_kernel, groups), grid=(rows // ti...  6.79 us

profile of v5, /device:TPU:0, one launch (start us, length us, event | category | flops | bytes accessed | tf_op | source)
XLA Modules:
  0.0 170.9 jit_solution(4123558801153237886)
XLA Ops:
  0.7 26.4 %ema_fwd.1 = (bf16[2048,512]{1,0:T(8,128)(2,1)}, bf16[2048,512]{1,0:T(8,128)(2,1)}, bf16[8,512,512]{2,1,0:T(8,128)(2,1)}, bf16[4,512,512]{2,1,0:T(8,128)(2,1)}, ...) custom-call(bf16[2048,512]{1,0:T(8,128)(2,1)} %tok.7, ...), custom_call_target="tpu_custom_call" | custom-call | tf_op jit(solution)/shard_map/ema_fwd/pallas_call | solution.py:354
  27.1 25.8 %forward_main.1 = (bf16[2048,512]{1,0:T(8,128)(2,1)}, bf16[2048,512]{1,0:T(8,128)(2,1)}, bf16[2048,512]{1,0:T(8,128)(2,1)}, bf16[2048,512]{1,0:T(8,128)(2,1)}, b...) custom-call(s32[2]{0:T(128)} %lens.1, ...), custom_call_target="tpu_custom_call" | custom-call | tf_op jit(solution)/shard_map/forward_main/pallas_call | solution.py:683
  52.8 20.3 %ffn_main.1 = (bf16[2048,512]{1,0:T(8,128)(2,1)}, bf16[2048,512]{1,0:T(8,128)(2,1)}, f32[4,8,128]{2,1,0:T(8,128)}, bf16[2,1024,128]{2,1,0:T(8,128)(2,1)}, bf16[2...) custom-call(s32[1]{0:T(128)} %bitcast.fs, ...), custom_call_target="tpu_custom_call" | custom-call | tf_op jit(solution)/shard_map/ffn_main/pallas_call | solution.py:753
  73.1 41.0 %backward_main.1 = (bf16[2048,512]{1,0:T(8,128)(2,1)}, bf16[2048,512]{1,0:T(8,128)(2,1)}, bf16[2048,512]{1,0:T(8,128)(2,1)}, bf16[2048,1024]{1,0:T(8,128)(2,1)},...) custom-call(bf16[2048,512]{1,0:T(8,128)(2,1)} %get-tuple-element.83., ...), custom_call_target="tpu_custom_call" | custom-call | tf_op jit(solution)/shard_map/backward_main/pallas_call | solution.py:963
  114.1 49.8 %input_main.1 = (bf16[4,2048,128]{2,1,0:T(8,128)(2,1)}, bf16[1024,128]{1,0:T(8,128)(2,1)}, bf16[1024,128]{1,0:T(8,128)(2,1)}, bf16[1536,128]{1,0:T(8,128)(2,1)},...) custom-call(bf16[2048,512]{1,0:T(8,128)(2,1)} %get-tuple-element.99.gh, ...), custom_call_target="tpu_custom_call" | custom-call | tf_op jit(solution)/shard_map/input_main/pallas_call | solution.py:1264
  163.9 6.8 %finish.1 = (bf16[2048,512]{1,0:T(8,128)(2,1)}, f32[2,128]{1,0:T(2,128)}, f32[4,16,128]{2,1,0:T(8,128)}, f32[4,32]{1,0:T(4,128)}, f32[256,512]{1,0:T(8,128)}, /*...) custom-call(s32[1]{0:T(128)} %bitcast.fs, ...), custom_call_target="tpu_custom_call" | custom-call | tf_op jit(solution)/shard_map/finish/pallas_call | solution.py:1315
